TPU v7x, 512 devices: a whole 4x8x8 slice. The times are simulated.
512 devices in a mesh: row: 16 (over x_hi, z), col: 16 (over y, x_lo), dp: 2 (over core).
Axes of the slice: x: 4 (x_hi: 2, x_lo: 2; x = x_hi * 2 + x_lo), y: 8, z: 8, core: 2. Of those that a mesh axis runs over, the one named last changes fastest.
Arguments:
- tokens: bfloat16 [512, 8192], P(('col', 'dp'), 'row'), may hold values from -6 to 6
- grad_out: bfloat16 [512, 8192], P(('col', 'dp'), 'row'), may hold values from -1.1953125 to 1.1953125
- gate_weight: bfloat16 [8192, 16384], P('row', 'col'), may hold values from -0.0625 to 0.0625
- up_weight: bfloat16 [8192, 16384], P('row', 'col'), may hold values from -0.0625 to 0.0625
- down_weight: bfloat16 [16384, 8192], P('col', 'row'), may hold values from -0.046875 to 0.046875
Outputs:
- grad_tokens: bfloat16 [512, 8192], P(('col', 'dp'), 'row')
- grad_gate: bfloat16 [8192, 16384], P('row', ('col', 'dp'))
- grad_up: bfloat16 [8192, 16384], P('row', ('col', 'dp'))
- grad_down: bfloat16 [16384, 8192], P(('col', 'dp'), 'row')
All inputs are finite; a program needn't handle non-finite values.
Results may differ from a plain program's by a relative error of at most 0.0049.
Values may be sent and summed in bfloat16 or wider, within the bound.
No kernel may reach another device: no remote copies, remote signals or barrier semaphores. Data moves between devices by JAX's collectives and lax.ppermute only.
A program may use at most 64 MiB of HBM per device.

v0:
```python
import jax
import jax.numpy as jnp
from jax import lax
from jax.sharding import PartitionSpec as P


def swiglu_back(gate, up, grad_hidden):
    sig = jax.nn.sigmoid(gate)
    hidden = (gate * sig * up).astype(jnp.bfloat16)
    grad_g = (grad_hidden * up * sig * (1.0 + gate * (1.0 - sig))).astype(jnp.bfloat16)
    grad_u = (grad_hidden * gate * sig).astype(jnp.bfloat16)
    return (hidden, grad_g, grad_u)


def body(tokens, grad_out, gate_weight, up_weight, down_weight):
    contract_last = (((1,), (1,)), ((), ()))
    contract_first = (((0,), (0,)), ((), ()))
    panel_in, panel_grad = (
        lax.all_gather(tokens, "col", axis=0, tiled=True),
        lax.all_gather(grad_out, "col", axis=0, tiled=True),
    )
    gate_part = jnp.dot(panel_in, gate_weight, preferred_element_type=jnp.float32)
    up_part = jnp.dot(panel_in, up_weight, preferred_element_type=jnp.float32)
    hidden_part = lax.dot_general(
        panel_grad, down_weight, contract_last, preferred_element_type=jnp.float32
    )
    gate, up, grad_hidden = lax.psum((gate_part, up_part, hidden_part), "row")
    hidden, grad_g, grad_u = swiglu_back(gate, up, grad_hidden)
    total = lax.dot_general(grad_g, gate_weight, contract_last, preferred_element_type=jnp.float32)
    grad_tokens = lax.psum_scatter(
        total
        + lax.dot_general(grad_u, up_weight, contract_last, preferred_element_type=jnp.float32),
        "col",
        scatter_dimension=0,
        tiled=True,
    ).astype(jnp.bfloat16)
    both_in, both_grad = (
        lax.all_gather(panel_in, "dp", axis=0, tiled=True),
        lax.all_gather(panel_grad, "dp", axis=0, tiled=True),
    )
    both_g, both_u, both_h = (
        lax.all_to_all(grad_g, "dp", split_axis=1, concat_axis=0, tiled=True),
        lax.all_to_all(grad_u, "dp", split_axis=1, concat_axis=0, tiled=True),
        lax.all_to_all(hidden, "dp", split_axis=1, concat_axis=0, tiled=True),
    )
    grad_gate = lax.dot_general(both_in, both_g, contract_first, preferred_element_type=jnp.float32)
    grad_up = lax.dot_general(both_in, both_u, contract_first, preferred_element_type=jnp.float32)
    grad_down = lax.dot_general(
        both_h, both_grad, contract_first, preferred_element_type=jnp.float32
    )
    return (
        grad_tokens,
        grad_gate.astype(jnp.bfloat16),
        grad_up.astype(jnp.bfloat16),
        grad_down.astype(jnp.bfloat16),
    )


def solution(mesh):
    in_specs = (
        P(("col", "dp"), "row"),
        P(("col", "dp"), "row"),
        P("row", "col"),
        P("row", "col"),
        P("col", "row"),
    )
    out_specs = (
        P(("col", "dp"), "row"),
        P("row", ("col", "dp")),
        P("row", ("col", "dp")),
        P(("col", "dp"), "row"),
    )
    return jax.shard_map(body, mesh=mesh, in_specs=in_specs, out_specs=out_specs, check_vma=False)
```

profile of v0, /device:TPU:4, one launch (start us, length us, event | category | flops | bytes accessed | tf_op | source)
XLA Modules:
  0.0 339.4 jit_solution(2064201888675651464)
XLA Ops:
  7.2 0.0 copy-start
  7.2 0.0 all-reduce.3.cloned.1.call-start
  7.2 35.4 %all_gather.13 = bf16[256,512]{1,0:T(8,128)(2,1)S(1)} all-gather(bf16[16,512]{1,0:T(8,128)(2,1)} %param.5), channel_id=1, replica_groups=mesh['row'=16,'col'=16,'dp'=2] {'col'}, dimensions={0}, use_global_device_ids=true | all-gather | bytes 278528 | tf_op jit(solution)/shard_map/all_gather | solution.py:19
  42.6 2.7 fusion.3
  45.3 0.0 copy-done
  45.3 0.0 copy-start.6
  45.3 0.0 copy-start.2
  45.3 1.4 fusion.4
  46.7 0.0 copy-done.6
  46.7 30.9 %all_gather.12 = bf16[256,512]{1,0:T(8,128)(2,1)S(1)} all-gather(bf16[16,512]{1,0:T(8,128)(2,1)S(1)} %copy-done.6), channel_id=1, replica_groups=mesh['row'=16,'col'=16,'dp'=2] {'col'}, dimensions={0}, use_global_device_ids=true | all-gather | bytes 278528 | tf_op jit(solution)/shard_map/all_gather | solution.py:20
  77.6 0.0 copy-done.2
  77.6 1.4 fusion.2
  79.1 0.0 all-reduce.3.cloned.1.call-update
  79.1 0.0 reduce-scatter.2.cloned.1.call-start
  79.1 176.2 %all-reduce.3.cloned.1.call-done = (f32[256,1024]{1,0:T(8,128)}, f32[256,1024]{1,0:T(8,128)}, f32[256,1024]{1,0:T(8,128)}) async-done(((f32[256,1024]{1,0:T(8,128)}, f32[256,1024]{1,0:T(8,128)}, f32[256,1024]{1,0:T(8,128)}), (f32[256,1024]{1,0:T(8,128)}, f32[256,1024]{1,0:T(8,128)}, f32[256,1024]{1,0:T(8,128)})) %all-reduce.3.cloned.1.call-update) | async-done | bytes 3145744 | tf_op jit(solution)/shard_map/psum | solution.py:27
  255.4 2.6 multiply_convert_fusion
  257.9 0.0 copy-start.1
  258.0 0.5 fusion.5
  258.4 0.7 copy-done.1
  259.2 1.3 convolution_add_fusion
  260.5 0.0 reduce-scatter.2.cloned.1.call-update
  260.5 2.2 all_gather.14
  262.7 0.0 copy-start.4
  262.7 2.3 all_gather.15
  265.0 4.2 %all_to_all.57 = bf16[256,2,512]{2,0,1:T(8,128)(2,1)S(1)} all-to-all(bf16[256,2,512]{2,0,1:T(8,128)(2,1)S(1)} %bitcast.44), channel_id=1, replica_groups=mesh['row'=16,'col'=16,'dp'=2] {'dp'}, dimensions={1} | all-to-all | bytes 1048576 | tf_op jit(solution)/shard_map/all_to_all | solution.py:42
  269.2 0.0 copy-done.4
  269.2 0.5 fusion
  269.6 1.0 copy.14
  270.7 0.0 copy-start.5
  270.7 4.3 %all_to_all.58 = bf16[256,2,512]{2,0,1:T(8,128)(2,1)S(1)} all-to-all(bf16[256,2,512]{2,0,1:T(8,128)(2,1)S(1)} %bitcast.45), channel_id=1, replica_groups=mesh['row'=16,'col'=16,'dp'=2] {'dp'}, dimensions={1} | all-to-all | bytes 1048576 | tf_op jit(solution)/shard_map/all_to_all | solution.py:43
  275.0 0.0 copy-done.5
  275.0 0.5 fusion.1
  275.4 1.0 copy.15
  276.5 0.0 copy-start.3
  276.5 4.3 %all_to_all.59 = bf16[256,2,512]{2,0,1:T(8,128)(2,1)S(1)} all-to-all(bf16[256,2,512]{2,0,1:T(8,128)(2,1)S(1)} %bitcast.46), channel_id=1, replica_groups=mesh['row'=16,'col'=16,'dp'=2] {'dp'}, dimensions={1} | all-to-all | bytes 1048576 | tf_op jit(solution)/shard_map/all_to_all | solution.py:44
  280.8 0.0 copy-done.3
  280.8 1.3 convolution_convert_fusion
  282.0 49.1 %reduce-scatter.2.cloned.1.call-done = f32[16,512]{1,0:T(8,128)} async-done(((f32[256,512]{1,0:T(8,128)}), f32[16,512]{1,0:T(8,128)}) %reduce-scatter.2.cloned.1.call-update) | async-done | bytes 32784 | tf_op jit(solution)/shard_map/reduce_scatter | solution.py:30
  331.2 1.4 convert_element_type.29
  (3 shorter events, 0.1 us)
Async XLA Ops:
  7.2 38.1 %copy-start = (bf16[512,1024]{1,0:T(8,128)(2,1)S(1)}, bf16[512,1024]{1,0:T(8,128)(2,1)}, u32[]{:S(2)}) copy-start(bf16[512,1024]{1,0:T(8,128)(2,1)} %param.7) | copy-start | bytes 3145732
  7.2 248.2 %all-reduce.3.cloned.1.call-start = ((), (), s32[]{:S(2)}) async-start(), calls=%async_computation.5 | async-start | bytes 6291456 | tf_op jit(solution)/shard_map/psum | solution.py:27
  45.3 1.4 copy-start.6
  45.3 32.3 %copy-start.2 = (bf16[1024,512]{1,0:T(8,128)(2,1)S(1)}, bf16[1024,512]{1,0:T(8,128)(2,1)}, u32[]{:S(2)}) copy-start(bf16[1024,512]{1,0:T(8,128)(2,1)} %param.9) | copy-start | bytes 3145732
  79.1 252.1 %reduce-scatter.2.cloned.1.call-start = ((), (), s32[]{:S(2)}) async-start(), calls=%async_computation.4 | async-start | bytes 557056 | tf_op jit(solution)/shard_map/reduce_scatter | solution.py:30
  257.9 1.2 copy-start.1
  262.7 6.5 %copy-start.4 = (bf16[512,512]{1,0:T(8,128)(2,1)}, bf16[512,512]{1,0:T(8,128)(2,1)S(1)}, u32[]{:S(2)}) copy-start(bf16[512,512]{1,0:T(8,128)(2,1)S(1)} %all_gather.14) | copy-start | bytes 1572868
  270.7 4.3 %copy-start.5 = (bf16[512,512]{1,0:T(8,128)(2,1)S(1)}, bf16[512,512]{1,0:T(8,128)(2,1)}, u32[]{:S(2)}) copy-start(bf16[512,512]{1,0:T(8,128)(2,1)} %copy-done.4) | copy-start | bytes 1572868
  276.5 4.3 %copy-start.3 = (bf16[512,512]{1,0:T(8,128)(2,1)S(1)}, bf16[512,512]{1,0:T(8,128)(2,1)}, u32[]{:S(2)}) copy-start(bf16[512,512]{1,0:T(8,128)(2,1)} %all_gather.15) | copy-start | bytes 1572868
Sparse Core Ops, SparseCore 0:
  79.2 176.1 all-reduce.2
  260.6 70.5 reduce-scatter.1
where the time goes:
time: 340 us; the launch traced here: 339 us
  waiting for transfers between devices  225 us (66%)
  blocking collectives  83.5 us (25%)
  between operations  14.1 us (4%)
  matrix products  9.46 us (3%)
  other arithmetic  3.94 us (1%)
    psum x1, waiting for transfers between devices, body(): gate, up, grad_hidden = lax.psum((gate_part, up_part, hidden_part), 'row')  176 us
    reduce_scatter x1, waiting for transfers between devices, body(): lax.psum_scatter(total + lax.dot_general(grad_u, up_weight, contract_last...  49.1 us
    all_gather x1, blocking collectives, body(): lax.all_gather(tokens, 'col', axis=0, tiled=True)  35.4 us
    all_gather x1, blocking collectives, body(): lax.all_gather(grad_out, 'col', axis=0, tiled=True)  30.9 us
  transfers between devices with their start and end apart: 2, of which 2 were waited for; matrix products, arithmetic and copies ran while one was open for 1% of the time, Pallas kernels for 0%

commit v1 on v0

v1 whole, which is shorter than its diff:
```python
import jax
import jax.numpy as jnp
from jax import lax
from jax.sharding import Mesh, PartitionSpec as P

ROW, COL = ("x_hi", "z"), ("y", "x_lo")
LAST = (((1,), (1,)), ((), ()))
FIRST = (((0,), (0,)), ((), ()))
SWAP = [(0, 1), (1, 0)]
f32, bf16 = jnp.float32, jnp.bfloat16


def swiglu_back(gate, up, grad_hidden):
    sig = jax.nn.sigmoid(gate)
    hidden = (gate * sig * up).astype(bf16)
    grad_g = (grad_hidden * up * sig * (1.0 + gate * (1.0 - sig))).astype(bf16)
    grad_u = (grad_hidden * gate * sig).astype(bf16)
    return hidden, grad_g, grad_u


def gather(x, axis, n):
    rows, cols = x.shape
    copies = jnp.broadcast_to(x[None], (n, rows, cols))
    return lax.all_to_all(copies, axis, 0, 0, tiled=True).reshape(n * rows, cols)


def scatter_sum(x, axis, n):
    rows, cols = x.shape
    blocks = lax.all_to_all(x.reshape(n, rows // n, cols), axis, 0, 0, tiled=True)
    return jnp.sum(blocks.astype(f32), axis=0)


def body(tokens, grad_out, gate_weight, up_weight, down_weight):
    x_hi, dp = lax.axis_index("x_hi"), lax.axis_index("dp")
    keep, send = dp * 512 + x_hi * 256, dp * 512 + (1 - x_hi) * 256

    def columns(at):
        return jnp.concatenate(
            [lax.dynamic_slice(w, (0, at), (512, 256)) for w in (gate_weight, up_weight)], axis=1
        )

    gu_keep, gu_send = columns(keep), columns(send)
    down_keep = lax.dynamic_slice(down_weight, (keep, 0), (256, 512))
    down_send = lax.dynamic_slice(down_weight, (send, 0), (256, 512))

    own_in = gather(tokens, COL, 16)
    own_grad = gather(grad_out, COL, 16)
    both_in = jnp.concatenate([own_in, lax.ppermute(own_in, "dp", SWAP)])
    both_grad = jnp.concatenate([own_grad, lax.ppermute(own_grad, "dp", SWAP)])

    def row_sum(x, w_keep, w_send, dims):
        sent = lax.dot_general(x, w_send, dims, preferred_element_type=f32).astype(bf16)
        got = lax.ppermute(sent, "x_hi", SWAP)
        part = lax.dot_general(x, w_keep, dims, preferred_element_type=f32) + got.astype(f32)
        return scatter_sum(part.astype(bf16), "z", 8)

    gu = row_sum(both_in, gu_keep, gu_send, (((1,), (0,)), ((), ())))
    grad_hidden = row_sum(both_grad, down_keep, down_send, LAST)
    hidden, grad_g, grad_u = swiglu_back(gu[:, :256], gu[:, 256:], grad_hidden)

    own_gu = gather(jnp.concatenate([grad_g, grad_u], axis=1), "z", 8)
    own_h = gather(hidden, "z", 8)
    far_gu = lax.ppermute(own_gu, "x_hi", SWAP)
    far_h = lax.ppermute(own_h, "x_hi", SWAP)

    total = lax.dot_general(own_gu, gu_keep, LAST, preferred_element_type=f32)
    total = total + lax.dot_general(far_gu, gu_send, LAST, preferred_element_type=f32)
    panel = total[:256] + lax.ppermute(total[256:], "dp", SWAP)
    grad_tokens = scatter_sum(panel.astype(bf16), COL, 16).astype(bf16)

    def both_halves(own, far):
        first = x_hi == 0
        return jnp.concatenate([jnp.where(first, own, far), jnp.where(first, far, own)], axis=1)

    all_g = both_halves(own_gu[:, :256], far_gu[:, :256])
    all_u = both_halves(own_gu[:, 256:], far_gu[:, 256:])
    all_h = both_halves(own_h, far_h)
    grad_gate = lax.dot_general(both_in, all_g, FIRST, preferred_element_type=f32)
    grad_up = lax.dot_general(both_in, all_u, FIRST, preferred_element_type=f32)
    grad_down = lax.dot_general(all_h, both_grad, FIRST, preferred_element_type=f32)
    return grad_tokens, grad_gate.astype(bf16), grad_up.astype(bf16), grad_down.astype(bf16)


def solution(mesh):
    fine = Mesh(mesh.devices.reshape(2, 8, 8, 2, 2), ("x_hi", "z", "y", "x_lo", "dp"))
    in_specs = (
        P(COL + ("dp",), ROW),
        P(COL + ("dp",), ROW),
        P(ROW, COL),
        P(ROW, COL),
        P(COL, ROW),
    )
    out_specs = (
        P(COL + ("dp",), ROW),
        P(ROW, COL + ("dp",)),
        P(ROW, COL + ("dp",)),
        P(COL + ("dp",), ROW),
    )
    return jax.shard_map(body, mesh=fine, in_specs=in_specs, out_specs=out_specs, check_vma=False)
```

time: 340 us -> 157 us (0.46)
  the two profiles are of different devices: /device:TPU:4 before, /device:TPU:1 now
where the time goes in v1:
time: 157 us; the launch traced here: 155 us
  starting transfers between devices  58.1 us (37%)
  waiting for transfers between devices  42.7 us (27%)
  blocking collectives  35.2 us (22%)
  matrix products  7.73 us (5%)
  local copies, waits for them, and re-layouts  6.11 us (4%)
  other arithmetic  3.74 us (2%)
    all_to_all x2, blocking collectives, gather(): lax.all_to_all(copies, axis, 0, 0, tiled=True).reshape(n * rows, cols)  35.2 us
    all_to_all x3, waiting for transfers between devices, scatter_sum(): lax.all_to_all(x.reshape(n, rows // n, cols), axis, 0, 0, tiled=True)  29.4 us
    all_to_all x3, starting transfers between devices, scatter_sum(): lax.all_to_all(x.reshape(n, rows // n, cols), axis, 0, 0, tiled=True)  17.3 us
    all_to_all x2, waiting for transfers between devices, gather(): lax.all_to_all(copies, axis, 0, 0, tiled=True).reshape(n * rows, cols)  10.3 us
    ppermute x1, starting transfers between devices, body(): panel = total[:256] + lax.ppermute(total[256:], 'dp', SWAP)  7.71 us
    all_to_all x2, starting transfers between devices, gather(): lax.all_to_all(copies, axis, 0, 0, tiled=True).reshape(n * rows, cols)  7.57 us
    ppermute x2, starting transfers between devices, row_sum(): got = lax.ppermute(sent, 'x_hi', SWAP)  6.76 us
    ppermute x1, starting transfers between devices, body(): both_in = jnp.concatenate([own_in, lax.ppermute(own_in, 'dp', SWAP)])  5.65 us
  transfers between devices with their start and end apart: 12, of which 7 were waited for; matrix products, arithmetic and copies ran while one was open for 7% of the time, Pallas kernels for 0%

profile of v1, /device:TPU:1, one launch (start us, length us, event | category | flops | bytes accessed | tf_op | source)
XLA Modules:
  0.0 154.6 jit_solution(13276382185153667998)
XLA Ops:
  0.6 0.0 copy-start
  0.6 0.8 broadcast_in_dim.8
  1.5 0.0 copy-start.10
  1.5 19.0 %all_to_all.35 = bf16[16,16,512]{2,1,0:T(8,128)(2,1)S(1)} all-to-all(bf16[16,16,512]{2,1,0:T(8,128)(2,1)S(1)} %broadcast_in_dim.8), channel_id=1, replica_groups=mesh['x_hi'=2,'z'=8,'y'=8,'x_lo'=2,'dp'=2] {'y','x_lo'}, dimensions={0} | all-to-all | bytes 524288 | tf_op jit(solution)/shard_map/all_to_all | solution.py:24
  20.5 0.0 copy-done.10
  20.5 0.8 broadcast_in_dim.9
  21.2 3.7 %all-to-all-start.2 = ((bf16[16,16,512]{2,1,0:T(8,128)(2,1)}), bf16[16,16,512]{2,1,0:T(8,128)(2,1)S(1)}, u32[]{:S(2)}, u32[]{:S(2)}) async-start(bf16[16,16,512]{2,1,0:T(8,128)(2,1)} %broadcast_in_dim.9), calls=%async_computation.2 | async-start | bytes 524288 | tf_op jit(solution)/shard_map/all_to_all | solution.py:24
  24.9 4.4 %collective-permute-start = (bf16[256,512]{1,0:T(8,128)(2,1)S(1)}, bf16[256,512]{1,0:T(8,128)(2,1)S(1)}, u32[]{:S(2)}, u32[]{:S(2)}) collective-permute-start(bf16[256,512]{1,0:T(8,128)(2,1)S(1)} %bitcast.20), channel_id=1, source_target_pairs={{0,1},{1,0},{2,3},{3,2},{4,5},{5,4},{6,7},{7,6},{8,9},{9,8},{10,11... | collective-permute-start | bytes 786440 | tf_op jit(solution)/shard_map/ppermute | solution.py:49
  29.3 5.1 %all-to-all-done.2 = bf16[16,16,512]{2,1,0:T(8,128)(2,1)S(1)} async-done(((bf16[16,16,512]{2,1,0:T(8,128)(2,1)}), bf16[16,16,512]{2,1,0:T(8,128)(2,1)S(1)}, u32[]{:S(2)}, u32[]{:S(2)}) %all-to-all-start.2) | async-done | bytes 262176 | tf_op jit(solution)/shard_map/all_to_all | solution.py:24
  34.5 5.6 %collective-permute-start.2 = (bf16[256,512]{1,0:T(8,128)(2,1)S(1)}, bf16[256,512]{1,0:T(8,128)(2,1)S(1)}, u32[]{:S(2)}, u32[]{:S(2)}) collective-permute-start(bf16[256,512]{1,0:T(8,128)(2,1)S(1)} %bitcast.15), channel_id=1, source_target_pairs={{0,1},{1,0},{2,3},{3,2},{4,5},{5,4},{6,7},{7,6},{8,9},{9,8},{10,11... | collective-permute-start | bytes 786440 | tf_op jit(solution)/shard_map/ppermute | solution.py:48
  40.1 0.0 collective-permute-done
  40.1 0.0 copy-done
  40.1 0.0 copy-start.14
  40.2 0.3 convolution_convert_fusion.4
  40.5 0.4 copy-done.14
  40.9 4.4 %collective-permute-start.1 = (bf16[512,256]{1,0:T(8,128)(2,1)S(1)}, bf16[512,256]{1,0:T(8,128)(2,1)S(1)}, u32[]{:S(2)}, u32[]{:S(2)}) collective-permute-start(bf16[512,256]{1,0:T(8,128)(2,1)S(1)} %convolution_convert_fusion.4), channel_id=1, source_target_pairs={{0,256},{256,0},{1,257},{257,1},{2,258},{258,2},{3,259},{259,3},{4... | collective-permute-start | bytes 786440 | tf_op jit(solution)/shard_map/ppermute | solution.py:53
  45.3 0.0 copy-done.9
  45.3 1.1 constant_dynamic-slice_fusion.2
  46.4 0.0 copy-start.1
  46.4 0.0 copy-start.3
  46.5 0.0 collective-permute-done.2
  46.5 0.0 copy-start.15
  46.5 0.4 convolution_convert_fusion.3
  46.9 0.2 copy-done.1
  47.1 0.1 copy-done.3
  47.2 0.1 copy-done.11
  47.3 2.4 %collective-permute-start.3 = (bf16[512,512]{1,0:T(8,128)(2,1)S(1)}, bf16[512,512]{1,0:T(8,128)(2,1)S(1)}, u32[]{:S(2)}, u32[]{:S(2)}) collective-permute-start(bf16[512,512]{1,0:T(8,128)(2,1)S(1)} %convolution_convert_fusion.3), channel_id=1, source_target_pairs={{0,256},{256,0},{1,257},{257,1},{2,258},{258,2},{3,259},{259,3},{4... | collective-permute-start | bytes 1572872 | tf_op jit(solution)/shard_map/ppermute | solution.py:53
  49.7 2.5 %collective-permute-done.1 = bf16[512,256]{1,0:T(8,128)(2,1)S(1)} collective-permute-done((bf16[512,256]{1,0:T(8,128)(2,1)S(1)}, bf16[512,256]{1,0:T(8,128)(2,1)S(1)}, u32[]{:S(2)}, u32[]{:S(2)}) %collective-permute-start.1) | collective-permute-done | bytes 262176 | tf_op jit(solution)/shard_map/ppermute | solution.py:53
  52.2 0.0 copy-done.15
  52.2 1.0 fusion.1
  53.2 10.2 %all-to-all-start.1 = ((bf16[8,64,256]{2,1,0:T(8,128)(2,1)}), bf16[8,64,256]{2,1,0:T(8,128)(2,1)S(1)}, u32[]{:S(2)}, u32[]{:S(2)}) async-start(bf16[8,64,256]{2,1,0:T(8,128)(2,1)} %bitcast.1), calls=%async_computation.1 | async-start | bytes 524288 | tf_op jit(solution)/shard_map/all_to_all | solution.py:29
  63.5 0.5 collective-permute-done.3
  64.0 0.0 copy-done.5
  64.0 1.2 fusion
  65.2 8.4 %all-to-all-done.1 = bf16[8,64,256]{2,1,0:T(8,128)(2,1)S(1)} async-done(((bf16[8,64,256]{2,1,0:T(8,128)(2,1)}), bf16[8,64,256]{2,1,0:T(8,128)(2,1)S(1)}, u32[]{:S(2)}, u32[]{:S(2)}) %all-to-all-start.1) | async-done | bytes 262176 | tf_op jit(solution)/shard_map/all_to_all | solution.py:29
  73.7 3.5 %all-to-all-start.3 = ((bf16[8,64,512]{2,1,0:T(8,128)(2,1)}), bf16[8,64,512]{2,1,0:T(8,128)(2,1)S(1)}, u32[]{:S(2)}, u32[]{:S(2)}) async-start(bf16[8,64,512]{2,1,0:T(8,128)(2,1)} %bitcast.3), calls=%async_computation.3 | async-start | bytes 1048576 | tf_op jit(solution)/shard_map/all_to_all | solution.py:29
  77.2 14.7 %all-to-all-done.3 = bf16[8,64,512]{2,1,0:T(8,128)(2,1)S(1)} async-done(((bf16[8,64,512]{2,1,0:T(8,128)(2,1)}), bf16[8,64,512]{2,1,0:T(8,128)(2,1)S(1)}, u32[]{:S(2)}, u32[]{:S(2)}) %all-to-all-start.3) | async-done | bytes 524320 | tf_op jit(solution)/shard_map/all_to_all | solution.py:29
  91.9 0.1 convert_reduce_fusion
  92.1 16.2 %all_to_all.36 = bf16[8,64,512]{2,1,0:T(8,128)(2,1)S(1)} all-to-all(bf16[8,64,512]{2,1,0:T(8,128)(2,1)S(1)} %broadcast_in_dim.10), channel_id=1, replica_groups=mesh['x_hi'=2,'z'=8,'y'=8,'x_lo'=2,'dp'=2] {'z'}, dimensions={0} | all-to-all | bytes 1048576 | tf_op jit(solution)/shard_map/all_to_all | solution.py:24
  108.3 0.7 broadcast_in_dim.11
  109.0 3.9 %all-to-all-start.6 = ((bf16[8,64,256]{2,1,0:T(8,128)(2,1)}), bf16[8,64,256]{2,1,0:T(8,128)(2,1)S(1)}, u32[]{:S(2)}, u32[]{:S(2)}) async-start(bf16[8,64,256]{2,1,0:T(8,128)(2,1)} %broadcast_in_dim.11), calls=%async_computation.6 | async-start | bytes 524288 | tf_op jit(solution)/shard_map/all_to_all | solution.py:24
  112.9 4.3 %collective-permute-start.4 = (bf16[512,512]{1,0:T(8,128)(2,1)S(1)}, bf16[512,512]{1,0:T(8,128)(2,1)S(1)}, u32[]{:S(2)}, u32[]{:S(2)}) collective-permute-start(bf16[512,512]{1,0:T(8,128)(2,1)S(1)} %bitcast.11), channel_id=1, source_target_pairs={{0,256},{256,0},{1,257},{257,1},{2,258},{258,2},{3,259},{259,3},{4... | collective-permute-start | bytes 1572872 | tf_op jit(solution)/shard_map/ppermute | solution.py:63
  117.2 5.1 %all-to-all-done.6 = bf16[8,64,256]{2,1,0:T(8,128)(2,1)S(1)} async-done(((bf16[8,64,256]{2,1,0:T(8,128)(2,1)}), bf16[8,64,256]{2,1,0:T(8,128)(2,1)S(1)}, u32[]{:S(2)}, u32[]{:S(2)}) %all-to-all-start.6) | async-done | bytes 262176 | tf_op jit(solution)/shard_map/all_to_all | solution.py:24
  122.4 4.4 %collective-permute-start.6 = (bf16[512,256]{1,0:T(8,128)(2,1)S(1)}, bf16[512,256]{1,0:T(8,128)(2,1)}, u32[]{:S(2)}, u32[]{:S(2)}) collective-permute-start(bf16[512,256]{1,0:T(8,128)(2,1)S(1)} %bitcast.14), channel_id=1, source_target_pairs={{0,256},{256,0},{1,257},{257,1},{2,258},{258,2},{3,259},{259,3},{4... | collective-permute-start | bytes 786440 | tf_op jit(solution)/shard_map/ppermute | solution.py:64
  126.8 0.5 fusion.12
  127.3 0.0 collective-permute-done.4
  127.3 0.5 convolution_add_fusion
  127.8 0.8 slice.35
  128.6 7.7 %collective-permute-start.5 = (f32[256,512]{1,0:T(8,128)}, f32[256,512]{1,0:T(8,128)}, u32[]{:S(2)}, u32[]{:S(2)}) collective-permute-start(f32[256,512]{1,0:T(8,128)} %slice.35), channel_id=1, source_target_pairs={{0,1},{1,0},{2,3},{3,2},{4,5},{5,4},{6,7},{7,6},{8,9},{9,8},{10,11... | collective-permute-start | bytes 1572872 | tf_op jit(solution)/shard_map/ppermute | solution.py:68
  136.4 0.0 copy-start.16
  136.4 0.0 collective-permute-done.6
  136.4 1.0 broadcast_select_fusion.1
  137.4 0.0 copy-done.16
  137.5 1.3 convolution_convert_fusion
  138.7 0.0 collective-permute-done.5
  138.7 1.8 %fusion.2 = bf16[256,512]{1,0:T(8,128)(2,1)} fusion(f32[256,512]{1,0:T(8,128)} %collective-permute-done.5, f32[512,512]{1,0:T(8,128)S(1)} %convolution_add_fusion), kind=kLoop, calls=%fused_computation.12 | loop fusion | flops 262144 | bytes 1310720 | tf_op jit(solution)/shard_map/convert_element_type | solution.py:69
  140.5 3.5 %all-to-all-start.5 = ((bf16[16,16,512]{2,1,0:T(8,128)(2,1)}), bf16[16,16,512]{2,1,0:T(8,128)(2,1)S(1)}, u32[]{:S(2)}, u32[]{:S(2)}) async-start(bf16[16,16,512]{2,1,0:T(8,128)(2,1)} %bitcast.5), calls=%async_computation.5 | async-start | bytes 524288 | tf_op jit(solution)/shard_map/all_to_all | solution.py:29
  144.1 0.1 broadcast_select_fusion.3
  144.2 0.8 copy-done.6
  145.0 0.1 copy-done.13
  145.1 1.3 convolution_convert_fusion.1
  146.3 1.3 convolution_convert_fusion.2
  147.6 6.3 %all-to-all-done.5 = bf16[16,16,512]{2,1,0:T(8,128)(2,1)S(1)} async-done(((bf16[16,16,512]{2,1,0:T(8,128)(2,1)}), bf16[16,16,512]{2,1,0:T(8,128)(2,1)S(1)}, u32[]{:S(2)}, u32[]{:S(2)}) %all-to-all-start.5) | async-done | bytes 262176 | tf_op jit(solution)/shard_map/all_to_all | solution.py:29
  153.9 0.6 reduce_sum.32
  (19 shorter events, 0.2 us)
Async XLA Ops:
  0.6 39.5 %copy-start = (bf16[1024,512]{1,0:T(8,128)(2,1)S(1)}, bf16[1024,512]{1,0:T(8,128)(2,1)}, u32[]{:S(2)}) copy-start(bf16[1024,512]{1,0:T(8,128)(2,1)} %param.9) | copy-start | bytes 3145732
  1.5 19.0 %copy-start.10 = (bf16[16,512]{1,0:T(8,128)(2,1)S(1)}, bf16[16,512]{1,0:T(8,128)(2,1)}, u32[]{:S(2)}) copy-start(bf16[16,512]{1,0:T(8,128)(2,1)} %param.5) | copy-start | bytes 49156
  20.5 31.7 %copy-start.7 = (bf16[16,16,512]{2,1,0:T(8,128)(2,1)}, bf16[16,16,512]{2,1,0:T(8,128)(2,1)S(1)}, u32[]{:S(2)}) copy-start(bf16[16,16,512]{2,1,0:T(8,128)(2,1)S(1)} %all_to_all.35) | copy-start | bytes 786436
  21.2 24.1 %copy-start.9 = (bf16[512,1024]{1,0:T(8,128)(2,1)S(1)}, bf16[512,1024]{1,0:T(8,128)(2,1)}, u32[]{:S(2)}) copy-start(bf16[512,1024]{1,0:T(8,128)(2,1)} %param.8) | copy-start | bytes 3145732
  21.2 13.2 %all-to-all-start.2 = ((bf16[16,16,512]{2,1,0:T(8,128)(2,1)}), bf16[16,16,512]{2,1,0:T(8,128)(2,1)S(1)}, u32[]{:S(2)}, u32[]{:S(2)}) async-start(bf16[16,16,512]{2,1,0:T(8,128)(2,1)} %broadcast_in_dim.9), calls=%async_computation.2 | async-start | bytes 524288 | tf_op jit(solution)/shard_map/all_to_all | solution.py:24
  24.9 15.2 %collective-permute-start = (bf16[256,512]{1,0:T(8,128)(2,1)S(1)}, bf16[256,512]{1,0:T(8,128)(2,1)S(1)}, u32[]{:S(2)}, u32[]{:S(2)}) collective-permute-start(bf16[256,512]{1,0:T(8,128)(2,1)S(1)} %bitcast.20), channel_id=1, source_target_pairs={{0,1},{1,0},{2,3},{3,2},{4,5},{5,4},{6,7},{7,6},{8,9},{9,8},{10,11... | collective-permute-start | bytes 786440 | tf_op jit(solution)/shard_map/ppermute | solution.py:49
  34.5 29.5 %copy-start.5 = (bf16[16,16,512]{2,1,0:T(8,128)(2,1)}, bf16[16,16,512]{2,1,0:T(8,128)(2,1)S(1)}, u32[]{:S(2)}) copy-start(bf16[16,16,512]{2,1,0:T(8,128)(2,1)S(1)} %all-to-all-done.2) | copy-start | bytes 786436
  34.5 12.0 %collective-permute-start.2 = (bf16[256,512]{1,0:T(8,128)(2,1)S(1)}, bf16[256,512]{1,0:T(8,128)(2,1)S(1)}, u32[]{:S(2)}, u32[]{:S(2)}) collective-permute-start(bf16[256,512]{1,0:T(8,128)(2,1)S(1)} %bitcast.15), channel_id=1, source_target_pairs={{0,1},{1,0},{2,3},{3,2},{4,5},{5,4},{6,7},{7,6},{8,9},{9,8},{10,11... | collective-permute-start | bytes 786440 | tf_op jit(solution)/shard_map/ppermute | solution.py:48
  40.1 0.7 copy-start.14
  40.9 11.3 %collective-permute-start.1 = (bf16[512,256]{1,0:T(8,128)(2,1)S(1)}, bf16[512,256]{1,0:T(8,128)(2,1)S(1)}, u32[]{:S(2)}, u32[]{:S(2)}) collective-permute-start(bf16[512,256]{1,0:T(8,128)(2,1)S(1)} %convolution_convert_fusion.4), channel_id=1, source_target_pairs={{0,256},{256,0},{1,257},{257,1},{2,258},{258,2},{3,259},{259,3},{4... | collective-permute-start | bytes 786440 | tf_op jit(solution)/shard_map/ppermute | solution.py:53
  46.4 0.7 copy-start.1
  46.4 0.8 copy-start.3
  46.5 0.9 copy-start.11
  46.5 5.7 %copy-start.15 = (bf16[256,512]{1,0:T(8,128)(2,1)S(1)}, bf16[256,512]{1,0:T(8,128)(2,1)}, u32[]{:S(2)}) copy-start(bf16[256,512]{1,0:T(8,128)(2,1)} %copy-done.14) | copy-start | bytes 786436
  47.3 16.6 %collective-permute-start.3 = (bf16[512,512]{1,0:T(8,128)(2,1)S(1)}, bf16[512,512]{1,0:T(8,128)(2,1)S(1)}, u32[]{:S(2)}, u32[]{:S(2)}) collective-permute-start(bf16[512,512]{1,0:T(8,128)(2,1)S(1)} %convolution_convert_fusion.3), channel_id=1, source_target_pairs={{0,256},{256,0},{1,257},{257,1},{2,258},{258,2},{3,259},{259,3},{4... | collective-permute-start | bytes 1572872 | tf_op jit(solution)/shard_map/ppermute | solution.py:53
  53.2 10.8 %copy-start.12 = (bf16[256,512]{1,0:T(8,128)(2,1)S(1)}, bf16[256,512]{1,0:T(8,128)(2,1)}, u32[]{:S(2)}) copy-start(bf16[256,512]{1,0:T(8,128)(2,1)} %copy-done.11) | copy-start | bytes 786436
  53.2 20.4 %all-to-all-start.1 = ((bf16[8,64,256]{2,1,0:T(8,128)(2,1)}), bf16[8,64,256]{2,1,0:T(8,128)(2,1)S(1)}, u32[]{:S(2)}, u32[]{:S(2)}) async-start(bf16[8,64,256]{2,1,0:T(8,128)(2,1)} %bitcast.1), calls=%async_computation.1 | async-start | bytes 524288 | tf_op jit(solution)/shard_map/all_to_all | solution.py:29
  73.7 18.2 %all-to-all-start.3 = ((bf16[8,64,512]{2,1,0:T(8,128)(2,1)}), bf16[8,64,512]{2,1,0:T(8,128)(2,1)S(1)}, u32[]{:S(2)}, u32[]{:S(2)}) async-start(bf16[8,64,512]{2,1,0:T(8,128)(2,1)} %bitcast.3), calls=%async_computation.3 | async-start | bytes 1048576 | tf_op jit(solution)/shard_map/all_to_all | solution.py:29
  109.0 13.3 %all-to-all-start.6 = ((bf16[8,64,256]{2,1,0:T(8,128)(2,1)}), bf16[8,64,256]{2,1,0:T(8,128)(2,1)S(1)}, u32[]{:S(2)}, u32[]{:S(2)}) async-start(bf16[8,64,256]{2,1,0:T(8,128)(2,1)} %broadcast_in_dim.11), calls=%async_computation.6 | async-start | bytes 524288 | tf_op jit(solution)/shard_map/all_to_all | solution.py:24
  112.9 14.4 %collective-permute-start.4 = (bf16[512,512]{1,0:T(8,128)(2,1)S(1)}, bf16[512,512]{1,0:T(8,128)(2,1)S(1)}, u32[]{:S(2)}, u32[]{:S(2)}) collective-permute-start(bf16[512,512]{1,0:T(8,128)(2,1)S(1)} %bitcast.11), channel_id=1, source_target_pairs={{0,256},{256,0},{1,257},{257,1},{2,258},{258,2},{3,259},{259,3},{4... | collective-permute-start | bytes 1572872 | tf_op jit(solution)/shard_map/ppermute | solution.py:63
  122.4 4.9 %copy-start.2 = (bf16[512,256]{1,0:T(8,128)(2,1)S(1)}, bf16[512,256]{1,0:T(8,128)(2,1)}, u32[]{:S(2)}) copy-start(bf16[512,256]{1,0:T(8,128)(2,1)} %copy-done.1) | copy-start | bytes 786436
  122.4 4.9 %copy-start.4 = (bf16[512,256]{1,0:T(8,128)(2,1)S(1)}, bf16[512,256]{1,0:T(8,128)(2,1)}, u32[]{:S(2)}) copy-start(bf16[512,256]{1,0:T(8,128)(2,1)} %copy-done.3) | copy-start | bytes 786436
  122.4 14.0 %collective-permute-start.6 = (bf16[512,256]{1,0:T(8,128)(2,1)S(1)}, bf16[512,256]{1,0:T(8,128)(2,1)}, u32[]{:S(2)}, u32[]{:S(2)}) collective-permute-start(bf16[512,256]{1,0:T(8,128)(2,1)S(1)} %bitcast.14), channel_id=1, source_target_pairs={{0,256},{256,0},{1,257},{257,1},{2,258},{258,2},{3,259},{259,3},{4... | collective-permute-start | bytes 786440 | tf_op jit(solution)/shard_map/ppermute | solution.py:64
  128.6 10.1 %collective-permute-start.5 = (f32[256,512]{1,0:T(8,128)}, f32[256,512]{1,0:T(8,128)}, u32[]{:S(2)}, u32[]{:S(2)}) collective-permute-start(f32[256,512]{1,0:T(8,128)} %slice.35), channel_id=1, source_target_pairs={{0,1},{1,0},{2,3},{3,2},{4,5},{5,4},{6,7},{7,6},{8,9},{9,8},{10,11... | collective-permute-start | bytes 1572872 | tf_op jit(solution)/shard_map/ppermute | solution.py:68
  136.3 1.1 copy-start.8
  136.4 1.1 copy-start.16
  140.5 13.4 %all-to-all-start.5 = ((bf16[16,16,512]{2,1,0:T(8,128)(2,1)}), bf16[16,16,512]{2,1,0:T(8,128)(2,1)S(1)}, u32[]{:S(2)}, u32[]{:S(2)}) async-start(bf16[16,16,512]{2,1,0:T(8,128)(2,1)} %bitcast.5), calls=%async_computation.5 | async-start | bytes 524288 | tf_op jit(solution)/shard_map/all_to_all | solution.py:29
  144.1 1.0 copy-start.6
  144.1 1.0 copy-start.13

commit v2 on v1

v2 whole, which is shorter than its diff:
```python
import jax
import jax.numpy as jnp
from jax import lax
from jax.experimental import pallas as pl
from jax.experimental.pallas import tpu as pltpu
from jax.sharding import Mesh, PartitionSpec as P

ROW, COL = ("x_hi", "z"), ("y", "x_lo")
PLAIN = (((1,), (0,)), ((), ()))
LAST = (((1,), (1,)), ((), ()))
FIRST = (((0,), (0,)), ((), ()))
SWAP = [(0, 1), (1, 0)]
f32, bf16 = jnp.float32, jnp.bfloat16


def swiglu_back(gate, up, grad_hidden):
    sig = jax.nn.sigmoid(gate)
    hidden = (gate * sig * up).astype(bf16)
    grad_g = (grad_hidden * up * sig * (1.0 + gate * (1.0 - sig))).astype(bf16)
    grad_u = (grad_hidden * gate * sig).astype(bf16)
    return hidden, grad_g, grad_u


def dot(a, b, dims):
    return lax.dot_general(a, b, dims, preferred_element_type=f32)


def gather(x, axis, n):
    rows, cols = x.shape
    copies = jnp.broadcast_to(x[None], (n, rows, cols))
    return lax.all_to_all(copies, axis, 0, 0, tiled=True).reshape(n * rows, cols)


def scatter_sum(x, axis, n):
    rows, cols = x.shape
    blocks = lax.all_to_all(x.reshape(n, rows // n, cols), axis, 0, 0, tiled=True)
    return jnp.sum(blocks.astype(f32), axis=0)


def gate_up_grads_kernel(x_hi, own, other, own_gu, far_gu, other_own, other_far, gate_ref, up_ref):
    def part(mine, others):
        total = dot(own[...], mine[:, :512], FIRST) + dot(other[...], others[...], FIRST)
        gate_ref[...] = total[:, :256].astype(bf16)
        up_ref[...] = total[:, 256:].astype(bf16)

    pl.when(pl.program_id(0) == 0)(lambda: part(own_gu, other_own))
    pl.when(pl.program_id(0) == 1)(lambda: part(far_gu, other_far))


def gate_up_grads(x_hi, own, other, own_gu, far_gu, other_own, other_far):
    whole = lambda shape: pl.BlockSpec(shape, lambda q, at: (0, 0))
    out = pl.BlockSpec((512, 256), lambda q, at: (0, at[0] ^ q))
    shape = jax.ShapeDtypeStruct((512, 512), bf16)
    return pl.pallas_call(
        gate_up_grads_kernel,
        out_shape=(shape, shape),
        grid_spec=pltpu.PrefetchScalarGridSpec(
            num_scalar_prefetch=1,
            grid=(2,),
            in_specs=[whole((256, 512)), whole((256, 512)), whole((256, 1024)), whole((256, 1024)),
                      whole((256, 512)), whole((256, 512))],
            out_specs=(out, out),
        ),
        compiler_params=pltpu.CompilerParams(vmem_limit_bytes=24 * 2**20),
        cost_estimate=pl.CostEstimate(flops=2 * 512**3 * 2, bytes_accessed=4 * 2**20, transcendentals=0),
    )(x_hi, own, other, own_gu, far_gu, other_own, other_far)


def down_grads_kernel(at, own, other, h, out_ref):
    total = dot(h[:, :256], own[...], FIRST) + dot(h[:, 256:], other[...], FIRST)
    out_ref[...] = total.astype(bf16)


def down_grads(at, own, other, h):
    half = lambda q, at: (0, 1)
    return pl.pallas_call(
        down_grads_kernel,
        out_shape=jax.ShapeDtypeStruct((512, 512), bf16),
        grid_spec=pltpu.PrefetchScalarGridSpec(
            num_scalar_prefetch=1,
            grid=(2,),
            in_specs=[pl.BlockSpec((256, 512), half), pl.BlockSpec((256, 512), half),
                      pl.BlockSpec((256, 512), lambda q, at: (0, q))],
            out_specs=pl.BlockSpec((256, 512), lambda q, at: (at[0] ^ q, 0)),
        ),
        compiler_params=pltpu.CompilerParams(vmem_limit_bytes=24 * 2**20),
        cost_estimate=pl.CostEstimate(flops=2 * 512**3, bytes_accessed=2 * 2**20, transcendentals=0),
    )(at, own, other, h)


def body(tokens, grad_out, gate_weight, up_weight, down_weight):
    x_hi, dp = lax.axis_index("x_hi"), lax.axis_index("dp")
    def quarter(x, core, side):
        return lax.dynamic_slice(x, (0, core * 512 + side * 256), (x.shape[0], 256))

    def gate_up(side):
        return jnp.concatenate(
            [quarter(w, core, side) for core in (dp, 1 - dp) for w in (gate_weight, up_weight)], axis=1
        )

    gu_keep, gu_send = gate_up(x_hi), gate_up(1 - x_hi)
    own = gather(jnp.concatenate([tokens, grad_out], axis=1), COL, 16)
    own, gu_keep, gu_send = lax.optimization_barrier((own, gu_keep, gu_send))
    own_in, own_grad = own[:, :512], own[:, 512:]

    got = lax.ppermute(dot(own_in, gu_send, PLAIN).astype(bf16), "x_hi", SWAP)
    gh_part = scatter_sum(dot(own_grad, down_weight, LAST).astype(bf16), "z", 8)

    def grad_hidden(side):
        return jnp.concatenate([quarter(gh_part, dp, side), quarter(gh_part, 1 - dp, side)], axis=1)

    gh = grad_hidden(x_hi) + lax.ppermute(grad_hidden(1 - x_hi), "x_hi", SWAP)
    other = lax.ppermute(own, "dp", SWAP)
    kept = lax.optimization_barrier(dot(own_in, gu_keep, PLAIN))
    got, other = lax.optimization_barrier((got, other))
    gu = scatter_sum((kept + got.astype(f32)).astype(bf16), "z", 8)
    gate = jnp.concatenate([gu[:, :256], gu[:, 512:768]], axis=1)
    up = jnp.concatenate([gu[:, 256:512], gu[:, 768:]], axis=1)
    hidden, g, u = swiglu_back(gate, up, gh)

    own_gu = gather(jnp.concatenate([g[:, :256], u[:, :256], g[:, 256:], u[:, 256:]], axis=1), "z", 8)
    hidden = jnp.concatenate([hidden[:, :256], lax.ppermute(hidden[:, 256:], "dp", SWAP)], axis=1)
    hidden = jnp.concatenate([hidden, lax.ppermute(hidden, "x_hi", SWAP)], axis=1)
    own_gu, hidden = lax.optimization_barrier((own_gu, hidden))
    all_h = gather(hidden, "z", 8)

    far_gu = lax.ppermute(own_gu, "x_hi", SWAP)
    other_own = lax.ppermute(own_gu[:, 512:], "dp", SWAP)
    far_gu, other_own = lax.optimization_barrier((far_gu, other_own))
    kept = lax.optimization_barrier(dot(own_gu, gu_keep, LAST))
    panel = (kept + dot(far_gu, gu_send, LAST)).astype(bf16)
    panel, far_gu = lax.optimization_barrier((panel, far_gu))
    grad_tokens = scatter_sum(panel, COL, 16).astype(bf16)

    other_far = lax.ppermute(far_gu[:, 512:], "dp", SWAP)
    at = x_hi.astype(jnp.int32)[None]
    grad_gate, grad_up = gate_up_grads(
        at, own, other, own_gu, far_gu, other_own, other_far
    )
    grad_down = down_grads(at, own, other, all_h)
    return grad_tokens, grad_gate, grad_up, grad_down


def solution(mesh):
    fine = Mesh(mesh.devices.reshape(2, 8, 8, 2, 2), ("x_hi", "z", "y", "x_lo", "dp"))
    in_specs = (
        P(COL + ("dp",), ROW),
        P(COL + ("dp",), ROW),
        P(ROW, COL),
        P(ROW, COL),
        P(COL, ROW),
    )
    out_specs = (
        P(COL + ("dp",), ROW),
        P(ROW, COL + ("dp",)),
        P(ROW, COL + ("dp",)),
        P(COL + ("dp",), ROW),
    )
    return jax.shard_map(body, mesh=fine, in_specs=in_specs, out_specs=out_specs, check_vma=False)
```

time: 157 us -> 138 us (0.88)
  blocking collectives: 35.2 us -> 0 us
  starting transfers between devices: 58.1 us -> 81.8 us
  waiting for transfers between devices: 42.7 us -> 33.7 us
  Pallas kernels: 0 us -> 3.26 us
  matrix products: 7.73 us -> 5.01 us
    all_to_all x2 -> x0, blocking collectives: 35.2 us -> none  [gather(): lax.all_to_all(copies, axis, 0, 0, tiled=True).reshape(n * rows, cols)]
    all_to_all x3, waiting for transfers between devices: 29.4 us -> 8.17 us  [scatter_sum(): lax.all_to_all(x.reshape(n, rows // n, cols), axis, 0, 0, tiled=True)]
    all_to_all x2 -> x3, starting transfers between devices: 7.57 us -> 18.7 us  [gather(): lax.all_to_all(copies, axis, 0, 0, tiled=True).reshape(n * rows, cols)]
    ppermute x6 -> x7, starting transfers between devices: 29 us -> 35.6 us  [the longest x1 7.7 us: body(): lax.ppermute(hidden[:, 256:], 'dp', SWAP)]
    all_to_all x3, starting transfers between devices: 17.3 us -> 23.1 us  [scatter_sum(): lax.all_to_all(x.reshape(n, rows // n, cols), axis, 0, 0, tiled=True)]
    ppermute x6 -> x7, waiting for transfers between devices: 2.99 us -> 8.33 us  [the longest x1 4.27 us: body(): got = lax.ppermute(dot(own_in, gu_send, PLAIN).astype(bf16), 'x_hi', SWAP)]
    ppermute x1, waiting for transfers between devices: 0.01 us -> 4.81 us  [body(): far_gu = lax.ppermute(own_gu, 'x_hi', SWAP)]
    pallas_call x0 -> x2, Pallas kernels: none -> 3.26 us  [the longest x1 1.79 us: gate_up_grads(): pl.pallas_call(gate_up_grads_kernel, out_shape=(shape, shape), grid_spec=...]
  transfers between devices with their start and end apart: 12 -> 14, of which waited for: 7 -> 7; matrix products, arithmetic and copies ran while one was open for 7% -> 6% of each run, Pallas kernels for 0% -> 2%
where the time goes in v2:
time: 138 us; the launch traced here: 136 us
  starting transfers between devices  81.8 us (59%)
  waiting for transfers between devices  33.7 us (24%)
  local copies, waits for them, and re-layouts  5.91 us (4%)
  matrix products  5.01 us (4%)
  other arithmetic  4.95 us (4%)
  Pallas kernels  3.26 us (2%)
    all_to_all x3, starting transfers between devices, scatter_sum(): lax.all_to_all(x.reshape(n, rows // n, cols), axis, 0, 0, tiled=True)  23.1 us
    all_to_all x3, starting transfers between devices, gather(): lax.all_to_all(copies, axis, 0, 0, tiled=True).reshape(n * rows, cols)  18.7 us
    all_to_all x3, waiting for transfers between devices, gather(): lax.all_to_all(copies, axis, 0, 0, tiled=True).reshape(n * rows, cols)  12.4 us
    all_to_all x3, waiting for transfers between devices, scatter_sum(): lax.all_to_all(x.reshape(n, rows // n, cols), axis, 0, 0, tiled=True)  8.17 us
    ppermute x1, starting transfers between devices, body(): lax.ppermute(hidden[:, 256:], 'dp', SWAP)  7.7 us
    ppermute x1, starting transfers between devices, body(): other_far = lax.ppermute(far_gu[:, 512:], 'dp', SWAP)  5.81 us
    dot_general x5, matrix products, dot(): return lax.dot_general(a, b, dims, preferred_element_type=f32)  5.01 us
    ppermute x1, starting transfers between devices, body(): other = lax.ppermute(own, 'dp', SWAP)  4.95 us
  transfers between devices with their start and end apart: 14, of which 7 were waited for; matrix products, arithmetic and copies ran while one was open for 6% of the time, Pallas kernels for 2%

profile of v2, /device:TPU:1, one launch (start us, length us, event | category | flops | bytes accessed | tf_op | source)
XLA Modules:
  0.0 135.6 jit_solution(7782626773268710946)
XLA Ops:
  0.6 0.0 copy-start
  0.6 0.0 copy-start.6
  0.7 0.9 pad_maximum_fusion.7
  1.5 0.9 broadcast_in_dim.8
  2.4 8.7 %all-to-all-start = ((bf16[16,16,1024]{2,1,0:T(8,128)(2,1)}), bf16[16,16,1024]{2,1,0:T(8,128)(2,1)S(1)}, u32[]{:S(2)}, u32[]{:S(2)}) async-start(bf16[16,16,1024]{2,1,0:T(8,128)(2,1)} %broadcast_in_dim.8), calls=%async_computation | async-start | bytes 1048576 | tf_op jit(solution)/shard_map/all_to_all | solution.py:31
  11.1 0.0 copy-done.6
  11.1 1.4 %constant_dynamic-slice_fusion.6 = (bf16[512,256]{1,0:T(8,128)(2,1)S(1)}, bf16[512,256]{1,0:T(8,128)(2,1)S(1)}, bf16[512,256]{1,0:T(8,128)(2,1)S(1)}, bf16[512,2...) fusion(bf16[512,1024]{1,0:T(8,128)(2,1)S(1)} %copy-done.6, ...), kind=kLoop, calls=%fused_computation.31 | loop fusion | bytes 4194320 | tf_op jit(solution)/shard_map/dynamic_slice | solution.py:94
  12.5 1.2 pad_maximum_fusion
  13.7 0.1 pad_maximum_fusion.1
  13.8 0.0 copy-start.3
  13.8 12.4 %all-to-all-done = bf16[16,16,1024]{2,1,0:T(8,128)(2,1)S(1)} async-done(((bf16[16,16,1024]{2,1,0:T(8,128)(2,1)}), bf16[16,16,1024]{2,1,0:T(8,128)(2,1)S(1)}, u32[]{:S(2)}, u32[]{:S(2)}) %all-to-all-start) | async-done | bytes 524320 | tf_op jit(solution)/shard_map/all_to_all | solution.py:31
  26.2 0.0 copy-done
  26.2 1.3 convolution_convert_fusion.1
  27.5 10.5 %all-to-all-start.1 = ((bf16[8,32,1024]{2,1,0:T(8,128)(2,1)}), bf16[8,32,1024]{2,1,0:T(8,128)(2,1)S(1)}, u32[]{:S(2)}, u32[]{:S(2)}) async-start(bf16[8,32,1024]{2,1,0:T(8,128)(2,1)} %bitcast.1), calls=%async_computation.1 | async-start | bytes 1048576 | tf_op jit(solution)/shard_map/all_to_all | solution.py:36
  38.0 0.0 copy-done.3
  38.0 0.0 copy-start.5
  38.0 0.4 convolution_convert_fusion
  38.5 4.4 %collective-permute-start.1 = (bf16[256,1024]{1,0:T(8,128)(2,1)S(1)}, bf16[256,1024]{1,0:T(8,128)(2,1)S(1)}, u32[]{:S(2)}, u32[]{:S(2)}) collective-permute-start(bf16[256,1024]{1,0:T(8,128)(2,1)S(1)} %convolution_convert_fusion), channel_id=1, source_target_pairs={{0,256},{256,0},{1,257},{257,1},{2,258},{258,2},{3,259},{259,3},{4... | collective-permute-start | bytes 1572872 | tf_op jit(solution)/shard_map/ppermute | solution.py:106
  42.8 5.0 %collective-permute-start.2 = (bf16[256,1024]{1,0:T(8,128)(2,1)S(1)}, bf16[256,1024]{1,0:T(8,128)(2,1)S(1)}, u32[]{:S(2)}, u32[]{:S(2)}) collective-permute-start(bf16[256,1024]{1,0:T(8,128)(2,1)S(1)} %bitcast.16), channel_id=1, source_target_pairs={{0,1},{1,0},{2,3},{3,2},{4,5},{5,4},{6,7},{7,6},{8,9},{9,8},{10,11... | collective-permute-start | bytes 1572872 | tf_op jit(solution)/shard_map/ppermute | solution.py:113
  47.8 0.0 copy-done.5
  47.8 0.4 fusion.3
  48.3 4.3 %collective-permute-done.1 = bf16[256,1024]{1,0:T(8,128)(2,1)S(1)} collective-permute-done((bf16[256,1024]{1,0:T(8,128)(2,1)S(1)}, bf16[256,1024]{1,0:T(8,128)(2,1)S(1)}, u32[]{:S(2)}, u32[]{:S(2)}) %collective-permute-start.1) | collective-permute-done | bytes 524320 | tf_op jit(solution)/shard_map/ppermute | solution.py:106
  52.5 0.0 collective-permute-done.2.other
  52.5 0.0 copy-start.1
  52.5 0.8 copy-done.1
  53.3 0.9 add_convert_fusion
  54.3 0.0 all-to-all-done.1
  54.3 6.4 %all-to-all-start.2 = ((bf16[8,32,1024]{2,1,0:T(8,128)(2,1)}), bf16[8,32,1024]{2,1,0:T(8,128)(2,1)S(1)}, u32[]{:S(2)}, u32[]{:S(2)}) async-start(bf16[8,32,1024]{2,1,0:T(8,128)(2,1)} %bitcast.2), calls=%async_computation.2 | async-start | bytes 1048576 | tf_op jit(solution)/shard_map/all_to_all | solution.py:36
  60.6 0.1 convert_reduce_fusion.1
  60.8 4.4 %collective-permute-start = (f32[32,512]{1,0:T(8,128)S(1)}, f32[32,512]{1,0:T(8,128)S(1)}, u32[]{:S(2)}, u32[]{:S(2)}) collective-permute-start(f32[32,512]{1,0:T(8,128)S(1)} %pad_maximum_fusion.2), channel_id=1, source_target_pairs={{0,256},{256,0},{1,257},{257,1},{2,258},{258,2},{3,259},{259,3},{4... | collective-permute-start | bytes 196616 | tf_op jit(solution)/shard_map/ppermute | solution.py:112
  65.1 8.2 %all-to-all-done.2 = bf16[8,32,1024]{2,1,0:T(8,128)(2,1)S(1)} async-done(((bf16[8,32,1024]{2,1,0:T(8,128)(2,1)}), bf16[8,32,1024]{2,1,0:T(8,128)(2,1)S(1)}, u32[]{:S(2)}, u32[]{:S(2)}) %all-to-all-start.2) | async-done | bytes 524320 | tf_op jit(solution)/shard_map/all_to_all | solution.py:36
  73.3 0.1 convert_reduce_fusion
  73.4 0.0 collective-permute-done
  73.4 0.1 multiply_convert_fusion.2
  73.5 0.9 broadcast_in_dim.9
  74.4 3.5 %all-to-all-start.3 = ((bf16[8,32,1024]{2,1,0:T(8,128)(2,1)}), bf16[8,32,1024]{2,1,0:T(8,128)(2,1)S(1)}, u32[]{:S(2)}, u32[]{:S(2)}) async-start(bf16[8,32,1024]{2,1,0:T(8,128)(2,1)} %broadcast_in_dim.9), calls=%async_computation.3 | async-start | bytes 1048576 | tf_op jit(solution)/shard_map/all_to_all | solution.py:31
  77.9 7.7 %collective-permute-start.3 = (bf16[32,256]{1,0:T(8,128)(2,1)S(1)}, bf16[32,256]{1,0:T(8,128)(2,1)S(1)}, u32[]{:S(2)}, u32[]{:S(2)}) collective-permute-start(bf16[32,256]{1,0:T(8,128)(2,1)S(1)} %get-tuple-element.50), channel_id=1, source_target_pairs={{0,1},{1,0},{2,3},{3,2},{4,5},{5,4},{6,7},{7,6},{8,9},{9,8},{10,11... | collective-permute-start | bytes 49160 | tf_op jit(solution)/shard_map/ppermute | solution.py:122
  85.6 0.8 collective-permute-done.3
  86.4 4.3 %collective-permute-start.4 = (bf16[32,512]{1,0:T(8,128)(2,1)S(1)}, bf16[32,512]{1,0:T(8,128)(2,1)S(1)}, u32[]{:S(2)}, u32[]{:S(2)}) collective-permute-start(bf16[32,512]{1,0:T(8,128)(2,1)S(1)} %pad_maximum_fusion.8), channel_id=1, source_target_pairs={{0,256},{256,0},{1,257},{257,1},{2,258},{258,2},{3,259},{259,3},{4... | collective-permute-start | bytes 98312 | tf_op jit(solution)/shard_map/ppermute | solution.py:123
  90.8 2.1 %collective-permute-done.4 = bf16[32,512]{1,0:T(8,128)(2,1)S(1)} collective-permute-done((bf16[32,512]{1,0:T(8,128)(2,1)S(1)}, bf16[32,512]{1,0:T(8,128)(2,1)S(1)}, u32[]{:S(2)}, u32[]{:S(2)}) %collective-permute-start.4) | collective-permute-done | bytes 32800 | tf_op jit(solution)/shard_map/ppermute | solution.py:123
  92.8 0.0 all-to-all-done.3
  92.9 0.9 broadcast_in_dim.11
  93.7 6.5 %all-to-all-start.5 = ((bf16[8,32,1024]{2,1,0:T(8,128)(2,1)}), bf16[8,32,1024]{2,1,0:T(8,128)(2,1)S(1)}, u32[]{:S(2)}, u32[]{:S(2)}) async-start(bf16[8,32,1024]{2,1,0:T(8,128)(2,1)} %broadcast_in_dim.11), calls=%async_computation.5 | async-start | bytes 1048576 | tf_op jit(solution)/shard_map/all_to_all | solution.py:31
  100.2 4.3 %collective-permute-start.5 = (bf16[256,1024]{1,0:T(8,128)(2,1)S(1)}, bf16[256,1024]{1,0:T(8,128)(2,1)S(1)}, u32[]{:S(2)}, u32[]{:S(2)}) collective-permute-start(bf16[256,1024]{1,0:T(8,128)(2,1)S(1)} %bitcast.20), channel_id=1, source_target_pairs={{0,256},{256,0},{1,257},{257,1},{2,258},{258,2},{3,259},{259,3},{4... | collective-permute-start | bytes 1572872 | tf_op jit(solution)/shard_map/ppermute | solution.py:127
  104.6 0.0 copy-start.4
  104.6 4.1 %collective-permute-start.6 = (bf16[256,512]{1,0:T(8,128)(2,1)S(1)}, bf16[256,512]{1,0:T(8,128)(2,1)S(1)}, u32[]{:S(2)}, u32[]{:S(2)}) collective-permute-start(bf16[256,512]{1,0:T(8,128)(2,1)S(1)} %slice.54), channel_id=1, source_target_pairs={{0,1},{1,0},{2,3},{3,2},{4,5},{5,4},{6,7},{7,6},{8,9},{9,8},{10,11... | collective-permute-start | bytes 786440 | tf_op jit(solution)/shard_map/ppermute | solution.py:128
  108.7 1.7 %fusion.9 = f32[256,512]{1,0:T(8,128)S(1)} fusion(bf16[256,1024]{1,0:T(8,128)(2,1)S(1)} %bitcast.22, bf16[512,1024]{1,0:T(8,128)(2,1)} %pad_maximum_fusion), kind=kOutput, calls=%fused_computation.41 | convolution fusion | flops 268435456 | bytes 2097152 | tf_op jit(solution)/shard_map/dot_general | solution.py:25
  110.4 0.0 collective-permute-done.6.other_own
  110.5 4.8 %collective-permute-done.5.far_gu = bf16[256,1024]{1,0:T(8,128)(2,1)S(1)} collective-permute-done((bf16[256,1024]{1,0:T(8,128)(2,1)S(1)}, bf16[256,1024]{1,0:T(8,128)(2,1)S(1)}, u32[]{:S(2)}, u32[]{:S(2)}) %collective-permute-start.5) | collective-permute-done | bytes 524320 | tf_op jit(solution)/shard_map/ppermute | solution.py:127
  115.3 0.0 copy-done.4
  115.3 1.2 fusion
  116.4 0.0 all-to-all-done.5
  116.4 6.2 %all-to-all-start.4 = ((bf16[16,16,512]{2,1,0:T(8,128)(2,1)}), bf16[16,16,512]{2,1,0:T(8,128)(2,1)}, u32[]{:S(2)}, u32[]{:S(2)}) async-start(bf16[16,16,512]{2,1,0:T(8,128)(2,1)} %bitcast.25), calls=%async_computation.4 | async-start | bytes 524288 | tf_op jit(solution)/shard_map/all_to_all | solution.py:36
  122.7 5.8 %collective-permute-start.7 = (bf16[256,512]{1,0:T(8,128)(2,1)S(1)}, bf16[256,512]{1,0:T(8,128)(2,1)S(1)}, u32[]{:S(2)}, u32[]{:S(2)}) collective-permute-start(bf16[256,512]{1,0:T(8,128)(2,1)S(1)} %slice.55), channel_id=1, source_target_pairs={{0,1},{1,0},{2,3},{3,2},{4,5},{5,4},{6,7},{7,6},{8,9},{9,8},{10,11... | collective-permute-start | bytes 786440 | tf_op jit(solution)/shard_map/ppermute | solution.py:135
  128.5 1.1 collective-permute-done.7.other_far
  129.6 0.0 copy-start.2
  129.6 1.0 copy-done.2
  130.7 1.8 %shard_map.84 = (bf16[512,512]{1,0:T(8,128)(2,1)}, bf16[512,512]{1,0:T(8,128)(2,1)}) custom-call(s32[1]{0:T(128)} %bitcast.5.x_hi.at, bf16[256,1024]{1,0:T(8,128)(2,1)S(1)} %bitcast.18, bf16[256,1024]{1,0:T(8,128)(2,1)S(1)} %copy-done.2, bf16[256,1024]{1,0:T(8,128)(2,1)S(1)} %bitcast.23, bf16[256,1024]{1,0:T(8,128)(2,1)S(1)} %collective-permute-done.5.far_gu, ...), custom_call_target="tpu_custom_call" | custom-call | flops 536870912 | bytes 4194304 | tf_op jit(solution)/shard_map/pallas_call | solution.py:54
  132.5 1.5 %shard_map.85 = bf16[512,512]{1,0:T(8,128)(2,1)} custom-call(s32[1]{0:T(128)} %bitcast.5.x_hi.at, bf16[256,1024]{1,0:T(8,128)(2,1)S(1)} %bitcast.19, bf16[256,1024]{1,0:T(8,128)(2,1)S(1)} %copy-done.2, bf16[256,1024]{1,0:T(8,128)(2,1)S(1)} %bitcast.24), custom_call_target="tpu_custom_call" | custom-call | flops 268435456 | bytes 2097152 | tf_op jit(solution)/shard_map/pallas_call | solution.py:76
  133.9 0.0 all-to-all-done.4
  133.9 1.6 %reduce_sum.32 = bf16[16,512]{1,0:T(8,128)(2,1)} reduce(bf16[16,16,512]{2,1,0:T(8,128)(2,1)} %all-to-all-done.4, bf16[]{:T(256)} %constant.23.clone.1), dimensions={0}, to_apply=%region_2.0 | reduce | flops 122880 | bytes 278530 | tf_op jit(solution)/shard_map/reduce_sum | solution.py:37
  (11 shorter events, 0.1 us)
Async XLA Ops:
  0.6 25.6 %copy-start = (bf16[1024,512]{1,0:T(8,128)(2,1)S(1)}, bf16[1024,512]{1,0:T(8,128)(2,1)}, u32[]{:S(2)}) copy-start(bf16[1024,512]{1,0:T(8,128)(2,1)} %param.9) | copy-start | bytes 3145732
  0.6 10.5 %copy-start.6 = (bf16[512,1024]{1,0:T(8,128)(2,1)S(1)}, bf16[512,1024]{1,0:T(8,128)(2,1)}, u32[]{:S(2)}) copy-start(bf16[512,1024]{1,0:T(8,128)(2,1)} %param.8) | copy-start | bytes 3145732
  2.4 23.8 %all-to-all-start = ((bf16[16,16,1024]{2,1,0:T(8,128)(2,1)}), bf16[16,16,1024]{2,1,0:T(8,128)(2,1)S(1)}, u32[]{:S(2)}, u32[]{:S(2)}) async-start(bf16[16,16,1024]{2,1,0:T(8,128)(2,1)} %broadcast_in_dim.8), calls=%async_computation | async-start | bytes 1048576 | tf_op jit(solution)/shard_map/all_to_all | solution.py:31
  13.8 24.2 %copy-start.3 = (bf16[512,1024]{1,0:T(8,128)(2,1)}, bf16[512,1024]{1,0:T(8,128)(2,1)S(1)}, u32[]{:S(2)}) copy-start(bf16[512,1024]{1,0:T(8,128)(2,1)S(1)} %pad_maximum_fusion.1) | copy-start | bytes 3145732
  27.5 26.8 %all-to-all-start.1 = ((bf16[8,32,1024]{2,1,0:T(8,128)(2,1)}), bf16[8,32,1024]{2,1,0:T(8,128)(2,1)S(1)}, u32[]{:S(2)}, u32[]{:S(2)}) async-start(bf16[8,32,1024]{2,1,0:T(8,128)(2,1)} %bitcast.1), calls=%async_computation.1 | async-start | bytes 1048576 | tf_op jit(solution)/shard_map/all_to_all | solution.py:36
  38.0 9.8 %copy-start.5 = (bf16[512,1024]{1,0:T(8,128)(2,1)S(1)}, bf16[512,1024]{1,0:T(8,128)(2,1)}, u32[]{:S(2)}) copy-start(bf16[512,1024]{1,0:T(8,128)(2,1)} %pad_maximum_fusion) | copy-start | bytes 3145732
  38.5 14.1 %collective-permute-start.1 = (bf16[256,1024]{1,0:T(8,128)(2,1)S(1)}, bf16[256,1024]{1,0:T(8,128)(2,1)S(1)}, u32[]{:S(2)}, u32[]{:S(2)}) collective-permute-start(bf16[256,1024]{1,0:T(8,128)(2,1)S(1)} %convolution_convert_fusion), channel_id=1, source_target_pairs={{0,256},{256,0},{1,257},{257,1},{2,258},{258,2},{3,259},{259,3},{4... | collective-permute-start | bytes 1572872 | tf_op jit(solution)/shard_map/ppermute | solution.py:106
  42.8 9.7 %collective-permute-start.2 = (bf16[256,1024]{1,0:T(8,128)(2,1)S(1)}, bf16[256,1024]{1,0:T(8,128)(2,1)S(1)}, u32[]{:S(2)}, u32[]{:S(2)}) collective-permute-start(bf16[256,1024]{1,0:T(8,128)(2,1)S(1)} %bitcast.16), channel_id=1, source_target_pairs={{0,1},{1,0},{2,3},{3,2},{4,5},{5,4},{6,7},{7,6},{8,9},{9,8},{10,11... | collective-permute-start | bytes 1572872 | tf_op jit(solution)/shard_map/ppermute | solution.py:113
  52.5 0.8 copy-start.1
  54.3 19.0 %all-to-all-start.2 = ((bf16[8,32,1024]{2,1,0:T(8,128)(2,1)}), bf16[8,32,1024]{2,1,0:T(8,128)(2,1)S(1)}, u32[]{:S(2)}, u32[]{:S(2)}) async-start(bf16[8,32,1024]{2,1,0:T(8,128)(2,1)} %bitcast.2), calls=%async_computation.2 | async-start | bytes 1048576 | tf_op jit(solution)/shard_map/all_to_all | solution.py:36
  60.8 12.6 %collective-permute-start = (f32[32,512]{1,0:T(8,128)S(1)}, f32[32,512]{1,0:T(8,128)S(1)}, u32[]{:S(2)}, u32[]{:S(2)}) collective-permute-start(f32[32,512]{1,0:T(8,128)S(1)} %pad_maximum_fusion.2), channel_id=1, source_target_pairs={{0,256},{256,0},{1,257},{257,1},{2,258},{258,2},{3,259},{259,3},{4... | collective-permute-start | bytes 196616 | tf_op jit(solution)/shard_map/ppermute | solution.py:112
  74.4 18.5 %all-to-all-start.3 = ((bf16[8,32,1024]{2,1,0:T(8,128)(2,1)}), bf16[8,32,1024]{2,1,0:T(8,128)(2,1)S(1)}, u32[]{:S(2)}, u32[]{:S(2)}) async-start(bf16[8,32,1024]{2,1,0:T(8,128)(2,1)} %broadcast_in_dim.9), calls=%async_computation.3 | async-start | bytes 1048576 | tf_op jit(solution)/shard_map/all_to_all | solution.py:31
  77.9 8.5 %collective-permute-start.3 = (bf16[32,256]{1,0:T(8,128)(2,1)S(1)}, bf16[32,256]{1,0:T(8,128)(2,1)S(1)}, u32[]{:S(2)}, u32[]{:S(2)}) collective-permute-start(bf16[32,256]{1,0:T(8,128)(2,1)S(1)} %get-tuple-element.50), channel_id=1, source_target_pairs={{0,1},{1,0},{2,3},{3,2},{4,5},{5,4},{6,7},{7,6},{8,9},{9,8},{10,11... | collective-permute-start | bytes 49160 | tf_op jit(solution)/shard_map/ppermute | solution.py:122
  86.4 6.4 %collective-permute-start.4 = (bf16[32,512]{1,0:T(8,128)(2,1)S(1)}, bf16[32,512]{1,0:T(8,128)(2,1)S(1)}, u32[]{:S(2)}, u32[]{:S(2)}) collective-permute-start(bf16[32,512]{1,0:T(8,128)(2,1)S(1)} %pad_maximum_fusion.8), channel_id=1, source_target_pairs={{0,256},{256,0},{1,257},{257,1},{2,258},{258,2},{3,259},{259,3},{4... | collective-permute-start | bytes 98312 | tf_op jit(solution)/shard_map/ppermute | solution.py:123
  93.7 22.7 %all-to-all-start.5 = ((bf16[8,32,1024]{2,1,0:T(8,128)(2,1)}), bf16[8,32,1024]{2,1,0:T(8,128)(2,1)S(1)}, u32[]{:S(2)}, u32[]{:S(2)}) async-start(bf16[8,32,1024]{2,1,0:T(8,128)(2,1)} %broadcast_in_dim.11), calls=%async_computation.5 | async-start | bytes 1048576 | tf_op jit(solution)/shard_map/all_to_all | solution.py:31
  100.2 15.0 %collective-permute-start.5 = (bf16[256,1024]{1,0:T(8,128)(2,1)S(1)}, bf16[256,1024]{1,0:T(8,128)(2,1)S(1)}, u32[]{:S(2)}, u32[]{:S(2)}) collective-permute-start(bf16[256,1024]{1,0:T(8,128)(2,1)S(1)} %bitcast.20), channel_id=1, source_target_pairs={{0,256},{256,0},{1,257},{257,1},{2,258},{258,2},{3,259},{259,3},{4... | collective-permute-start | bytes 1572872 | tf_op jit(solution)/shard_map/ppermute | solution.py:127
  104.6 10.6 %copy-start.4 = (bf16[512,1024]{1,0:T(8,128)(2,1)S(1)}, bf16[512,1024]{1,0:T(8,128)(2,1)}, u32[]{:S(2)}) copy-start(bf16[512,1024]{1,0:T(8,128)(2,1)} %copy-done.3) | copy-start | bytes 3145732
  104.6 5.8 %collective-permute-start.6 = (bf16[256,512]{1,0:T(8,128)(2,1)S(1)}, bf16[256,512]{1,0:T(8,128)(2,1)S(1)}, u32[]{:S(2)}, u32[]{:S(2)}) collective-permute-start(bf16[256,512]{1,0:T(8,128)(2,1)S(1)} %slice.54), channel_id=1, source_target_pairs={{0,1},{1,0},{2,3},{3,2},{4,5},{5,4},{6,7},{7,6},{8,9},{9,8},{10,11... | collective-permute-start | bytes 786440 | tf_op jit(solution)/shard_map/ppermute | solution.py:128
  116.4 17.5 %all-to-all-start.4 = ((bf16[16,16,512]{2,1,0:T(8,128)(2,1)}), bf16[16,16,512]{2,1,0:T(8,128)(2,1)}, u32[]{:S(2)}, u32[]{:S(2)}) async-start(bf16[16,16,512]{2,1,0:T(8,128)(2,1)} %bitcast.25), calls=%async_computation.4 | async-start | bytes 524288 | tf_op jit(solution)/shard_map/all_to_all | solution.py:36
  122.7 7.0 %collective-permute-start.7 = (bf16[256,512]{1,0:T(8,128)(2,1)S(1)}, bf16[256,512]{1,0:T(8,128)(2,1)S(1)}, u32[]{:S(2)}, u32[]{:S(2)}) collective-permute-start(bf16[256,512]{1,0:T(8,128)(2,1)S(1)} %slice.55), channel_id=1, source_target_pairs={{0,1},{1,0},{2,3},{3,2},{4,5},{5,4},{6,7},{7,6},{8,9},{9,8},{10,11... | collective-permute-start | bytes 786440 | tf_op jit(solution)/shard_map/ppermute | solution.py:135
  129.6 1.0 copy-start.2

commit v3 on v2

--- a/solution.py
+++ b/solution.py
@@ -25,16 +25,24 @@
     return lax.dot_general(a, b, dims, preferred_element_type=f32)
 
 
+Z_ORDER = (0, 4, 7, 3, 1, 5, 6, 2)
+COL_ORDER = (7, 0, 6, 2, 14, 12, 15, 8, 13, 4, 1, 9, 3, 11, 10, 5)
+
+
+def exchange(x, axis):
+    order = Z_ORDER if axis == "z" else COL_ORDER
+    return lax.all_to_all(x, axis, 0, 0, tiled=True, axis_index_groups=[list(order)])
+
+
 def gather(x, axis, n):
     rows, cols = x.shape
     copies = jnp.broadcast_to(x[None], (n, rows, cols))
-    return lax.all_to_all(copies, axis, 0, 0, tiled=True).reshape(n * rows, cols)
+    return exchange(copies, axis).reshape(n * rows, cols)
 
 
 def scatter_sum(x, axis, n):
     rows, cols = x.shape
-    blocks = lax.all_to_all(x.reshape(n, rows // n, cols), axis, 0, 0, tiled=True)
-    return jnp.sum(blocks.astype(f32), axis=0)
+    return jnp.sum(exchange(x.reshape(n, rows // n, cols), axis).astype(f32), axis=0)
 
 
 def gate_up_grads_kernel(x_hi, own, other, own_gu, far_gu, other_own, other_far, gate_ref, up_ref):
@@ -66,26 +74,29 @@
     )(x_hi, own, other, own_gu, far_gu, other_own, other_far)
 
 
-def down_grads_kernel(at, own, other, h, out_ref):
-    total = dot(h[:, :256], own[...], FIRST) + dot(h[:, 256:], other[...], FIRST)
-    out_ref[...] = total.astype(bf16)
+def down_grads_kernel(x_hi, own, other, own_h, far_h, out_ref):
+    def part(h):
+        total = dot(h[:, :256], own[...], FIRST) + dot(h[:, 256:], other[...], FIRST)
+        out_ref[...] = total.astype(bf16)
+
+    pl.when(pl.program_id(0) == 0)(lambda: part(own_h))
+    pl.when(pl.program_id(0) == 1)(lambda: part(far_h))
 
 
-def down_grads(at, own, other, h):
-    half = lambda q, at: (0, 1)
+def down_grads(x_hi, own, other, own_h, far_h):
+    half = lambda column: pl.BlockSpec((256, 512), lambda q, at: (0, column))
     return pl.pallas_call(
         down_grads_kernel,
         out_shape=jax.ShapeDtypeStruct((512, 512), bf16),
         grid_spec=pltpu.PrefetchScalarGridSpec(
             num_scalar_prefetch=1,
             grid=(2,),
-            in_specs=[pl.BlockSpec((256, 512), half), pl.BlockSpec((256, 512), half),
-                      pl.BlockSpec((256, 512), lambda q, at: (0, q))],
+            in_specs=[half(1), half(1), half(0), half(0)],
             out_specs=pl.BlockSpec((256, 512), lambda q, at: (at[0] ^ q, 0)),
         ),
         compiler_params=pltpu.CompilerParams(vmem_limit_bytes=24 * 2**20),
         cost_estimate=pl.CostEstimate(flops=2 * 512**3, bytes_accessed=2 * 2**20, transcendentals=0),
-    )(at, own, other, h)
+    )(x_hi, own, other, own_h, far_h)
 
 
 def body(tokens, grad_out, gate_weight, up_weight, down_weight):
@@ -120,24 +131,24 @@
 
     own_gu = gather(jnp.concatenate([g[:, :256], u[:, :256], g[:, 256:], u[:, 256:]], axis=1), "z", 8)
     hidden = jnp.concatenate([hidden[:, :256], lax.ppermute(hidden[:, 256:], "dp", SWAP)], axis=1)
-    hidden = jnp.concatenate([hidden, lax.ppermute(hidden, "x_hi", SWAP)], axis=1)
-    own_gu, hidden = lax.optimization_barrier((own_gu, hidden))
-    all_h = gather(hidden, "z", 8)
+    copies = jnp.broadcast_to(hidden[None], (8, 32, 512))
+    own_gu, copies = lax.optimization_barrier((own_gu, copies))
+    own_h = exchange(copies, "z").reshape(256, 512)
+    far_h = lax.ppermute(own_h, "x_hi", SWAP)
 
     far_gu = lax.ppermute(own_gu, "x_hi", SWAP)
-    other_own = lax.ppermute(own_gu[:, 512:], "dp", SWAP)
-    far_gu, other_own = lax.optimization_barrier((far_gu, other_own))
     kept = lax.optimization_barrier(dot(own_gu, gu_keep, LAST))
     panel = (kept + dot(far_gu, gu_send, LAST)).astype(bf16)
-    panel, far_gu = lax.optimization_barrier((panel, far_gu))
+    panel, far_gu, own_gu = lax.optimization_barrier((panel, far_gu, own_gu))
     grad_tokens = scatter_sum(panel, COL, 16).astype(bf16)
 
+    other_own = lax.ppermute(own_gu[:, 512:], "dp", SWAP)
     other_far = lax.ppermute(far_gu[:, 512:], "dp", SWAP)
     at = x_hi.astype(jnp.int32)[None]
     grad_gate, grad_up = gate_up_grads(
         at, own, other, own_gu, far_gu, other_own, other_far
     )
-    grad_down = down_grads(at, own, other, all_h)
+    grad_down = down_grads(at, own, other, own_h, far_h)
     return grad_tokens, grad_gate, grad_up, grad_down
 
 

time: 138 us -> 134 us (0.971); the launches traced: 136 us -> 133 us
  starting transfers between devices: 81.8 us -> 78.6 us
  waiting for transfers between devices: 33.7 us -> 36.3 us
  local copies, waits for them, and re-layouts: 5.91 us -> 3.95 us
    all_to_all x6, waiting for transfers between devices: 20.6 us -> 24.7 us  [exchange(): lax.all_to_all(x, axis, 0, 0, tiled=True, axis_index_groups=[list(order)])]
    ppermute x1, starting transfers between devices: 5.81 us -> 1.92 us  [body(): other_far = lax.ppermute(far_gu[:, 512:], 'dp', SWAP)]
    ppermute x1, starting transfers between devices: 7.7 us -> 5.07 us  [body(): lax.ppermute(hidden[:, 256:], 'dp', SWAP)]
    ppermute x1, waiting for transfers between devices: 2.09 us -> 0.01 us  [body(): far_h = lax.ppermute(own_h, 'x_hi', SWAP)]
    all_to_all x6, starting transfers between devices: 41.8 us -> 43.7 us  [exchange(): lax.all_to_all(x, axis, 0, 0, tiled=True, axis_index_groups=[list(order)])]
    unnamed x14 -> x10, local copies, waits for them, and re-layouts: 1.86 us -> 0.03 us
  transfers between devices with their start and end apart: 14 -> 14, of which waited for: 7 -> 6; matrix products, arithmetic and copies ran while one was open for 6% -> 6% of each run, Pallas kernels for 2% -> 2%
where the time goes in v3:
time: 134 us; the launch traced here: 133 us
  starting transfers between devices  78.6 us (59%)
  waiting for transfers between devices  36.3 us (27%)
  matrix products  5.11 us (4%)
  other arithmetic  4.92 us (4%)
  local copies, waits for them, and re-layouts  3.95 us (3%)
  Pallas kernels  3.25 us (2%)
    all_to_all x6, starting transfers between devices, exchange(): lax.all_to_all(x, axis, 0, 0, tiled=True, axis_index_groups=[list(order)])  43.7 us
    all_to_all x6, waiting for transfers between devices, exchange(): lax.all_to_all(x, axis, 0, 0, tiled=True, axis_index_groups=[list(order)])  24.7 us
    ppermute x1, waiting for transfers between devices, body(): got = lax.ppermute(dot(own_in, gu_send, PLAIN).astype(bf16), 'x_hi', SWAP)  5.6 us
    ppermute x1, starting transfers between devices, body(): other_own = lax.ppermute(own_gu[:, 512:], 'dp', SWAP)  5.26 us
    ppermute x1, waiting for transfers between devices, body(): far_gu = lax.ppermute(own_gu, 'x_hi', SWAP)  5.13 us
    dot_general x5, matrix products, dot(): return lax.dot_general(a, b, dims, preferred_element_type=f32)  5.11 us
    ppermute x1, starting transfers between devices, body(): lax.ppermute(hidden[:, 256:], 'dp', SWAP)  5.07 us
    ppermute x1, starting transfers between devices, body(): gh = grad_hidden(x_hi) + lax.ppermute(grad_hidden(1 - x_hi), 'x_hi', SWAP)  4.62 us
  transfers between devices with their start and end apart: 14, of which 6 were waited for; matrix products, arithmetic and copies ran while one was open for 6% of the time, Pallas kernels for 2%

profile of v3, /device:TPU:1, one launch (start us, length us, event | category | flops | bytes accessed | tf_op | source)
XLA Modules:
  0.0 133.0 jit_solution(12782155658637993675)
XLA Ops:
  0.6 0.0 copy-start
  0.6 0.0 copy-start.4
  0.7 0.9 pad_maximum_fusion.6
  1.5 0.9 broadcast_in_dim.8
  2.4 9.2 %all-to-all-start = ((bf16[16,16,1024]{2,1,0:T(8,128)(2,1)}), bf16[16,16,1024]{2,1,0:T(8,128)(2,1)S(1)}, u32[]{:S(2)}, u32[]{:S(2)}) async-start(bf16[16,16,1024]{2,1,0:T(8,128)(2,1)} %broadcast_in_dim.8), calls=%async_computation | async-start | bytes 1048576 | tf_op jit(solution)/shard_map/all_to_all | solution.py:34
  11.6 0.0 copy-done.4
  11.6 1.4 %constant_dynamic-slice_fusion.6 = (bf16[512,256]{1,0:T(8,128)(2,1)S(1)}, bf16[512,256]{1,0:T(8,128)(2,1)S(1)}, bf16[512,256]{1,0:T(8,128)(2,1)S(1)}, bf16[512,2...) fusion(bf16[512,1024]{1,0:T(8,128)(2,1)S(1)} %copy-done.4, ...), kind=kLoop, calls=%fused_computation.30 | loop fusion | bytes 4194320 | tf_op jit(solution)/shard_map/dynamic_slice | solution.py:105
  13.0 1.1 pad_maximum_fusion
  14.2 0.1 pad_maximum_fusion.1
  14.3 0.0 copy-start.1
  14.3 8.1 %all-to-all-done = bf16[16,16,1024]{2,1,0:T(8,128)(2,1)S(1)} async-done(((bf16[16,16,1024]{2,1,0:T(8,128)(2,1)}), bf16[16,16,1024]{2,1,0:T(8,128)(2,1)S(1)}, u32[]{:S(2)}, u32[]{:S(2)}) %all-to-all-start) | async-done | bytes 524320 | tf_op jit(solution)/shard_map/all_to_all | solution.py:34
  22.4 0.0 copy-done
  22.4 1.3 convolution_convert_fusion.1
  23.7 12.6 %all-to-all-start.1 = ((bf16[8,32,1024]{2,1,0:T(8,128)(2,1)}), bf16[8,32,1024]{2,1,0:T(8,128)(2,1)S(1)}, u32[]{:S(2)}, u32[]{:S(2)}) async-start(bf16[8,32,1024]{2,1,0:T(8,128)(2,1)} %bitcast.1), calls=%async_computation.1 | async-start | bytes 1048576 | tf_op jit(solution)/shard_map/all_to_all | solution.py:34
  36.3 0.0 copy-done.1
  36.4 0.0 copy-start.3
  36.4 0.4 convolution_convert_fusion
  36.8 4.6 %collective-permute-start.1 = (bf16[256,1024]{1,0:T(8,128)(2,1)S(1)}, bf16[256,1024]{1,0:T(8,128)(2,1)S(1)}, u32[]{:S(2)}, u32[]{:S(2)}) collective-permute-start(bf16[256,1024]{1,0:T(8,128)(2,1)S(1)} %convolution_convert_fusion), channel_id=1, source_target_pairs={{0,256},{256,0},{1,257},{257,1},{2,258},{258,2},{3,259},{259,3},{4... | collective-permute-start | bytes 1572872 | tf_op jit(solution)/shard_map/ppermute | solution.py:117
  41.4 4.2 %collective-permute-start.2 = (bf16[256,1024]{1,0:T(8,128)(2,1)S(1)}, bf16[256,1024]{1,0:T(8,128)(2,1)S(1)}, u32[]{:S(2)}, u32[]{:S(2)}) collective-permute-start(bf16[256,1024]{1,0:T(8,128)(2,1)S(1)} %bitcast.16), channel_id=1, source_target_pairs={{0,1},{1,0},{2,3},{3,2},{4,5},{5,4},{6,7},{7,6},{8,9},{9,8},{10,11... | collective-permute-start | bytes 1572872 | tf_op jit(solution)/shard_map/ppermute | solution.py:124
  45.6 0.0 copy-done.3
  45.6 0.4 fusion.3
  46.1 5.6 %collective-permute-done.1 = bf16[256,1024]{1,0:T(8,128)(2,1)S(1)} collective-permute-done((bf16[256,1024]{1,0:T(8,128)(2,1)S(1)}, bf16[256,1024]{1,0:T(8,128)(2,1)S(1)}, u32[]{:S(2)}, u32[]{:S(2)}) %collective-permute-start.1) | collective-permute-done | bytes 524320 | tf_op jit(solution)/shard_map/ppermute | solution.py:117
  51.7 0.0 collective-permute-done.2.other
  51.7 0.9 add_convert_fusion
  52.6 0.0 all-to-all-done.1
  52.6 6.4 %all-to-all-start.2 = ((bf16[8,32,1024]{2,1,0:T(8,128)(2,1)}), bf16[8,32,1024]{2,1,0:T(8,128)(2,1)S(1)}, u32[]{:S(2)}, u32[]{:S(2)}) async-start(bf16[8,32,1024]{2,1,0:T(8,128)(2,1)} %bitcast.26), calls=%async_computation.2 | async-start | bytes 1048576 | tf_op jit(solution)/shard_map/all_to_all | solution.py:34
  59.0 0.1 convert_reduce_fusion.1
  59.1 4.6 %collective-permute-start = (f32[32,512]{1,0:T(8,128)S(1)}, f32[32,512]{1,0:T(8,128)S(1)}, u32[]{:S(2)}, u32[]{:S(2)}) collective-permute-start(f32[32,512]{1,0:T(8,128)S(1)} %pad_maximum_fusion.2), channel_id=1, source_target_pairs={{0,256},{256,0},{1,257},{257,1},{2,258},{258,2},{3,259},{259,3},{4... | collective-permute-start | bytes 196616 | tf_op jit(solution)/shard_map/ppermute | solution.py:123
  63.7 8.9 %all-to-all-done.2 = bf16[8,32,1024]{2,1,0:T(8,128)(2,1)S(1)} async-done(((bf16[8,32,1024]{2,1,0:T(8,128)(2,1)}), bf16[8,32,1024]{2,1,0:T(8,128)(2,1)S(1)}, u32[]{:S(2)}, u32[]{:S(2)}) %all-to-all-start.2) | async-done | bytes 524320 | tf_op jit(solution)/shard_map/all_to_all | solution.py:34
  72.7 0.1 convert_reduce_fusion
  72.8 0.0 collective-permute-done
  72.8 0.1 multiply_convert_fusion.2
  72.9 0.9 broadcast_in_dim.9
  73.7 3.5 %all-to-all-start.3 = ((bf16[8,32,1024]{2,1,0:T(8,128)(2,1)}), bf16[8,32,1024]{2,1,0:T(8,128)(2,1)S(1)}, u32[]{:S(2)}, u32[]{:S(2)}) async-start(bf16[8,32,1024]{2,1,0:T(8,128)(2,1)} %broadcast_in_dim.9), calls=%async_computation.3 | async-start | bytes 1048576 | tf_op jit(solution)/shard_map/all_to_all | solution.py:34
  77.2 5.1 %collective-permute-start.3 = (bf16[32,256]{1,0:T(8,128)(2,1)S(1)}, bf16[32,256]{1,0:T(8,128)(2,1)S(1)}, u32[]{:S(2)}, u32[]{:S(2)}) collective-permute-start(bf16[32,256]{1,0:T(8,128)(2,1)S(1)} %get-tuple-element.48), channel_id=1, source_target_pairs={{0,1},{1,0},{2,3},{3,2},{4,5},{5,4},{6,7},{7,6},{8,9},{9,8},{10,11... | collective-permute-start | bytes 49160 | tf_op jit(solution)/shard_map/ppermute | solution.py:133
  82.3 0.8 collective-permute-done.3
  83.1 7.7 %all-to-all-done.3 = bf16[8,32,1024]{2,1,0:T(8,128)(2,1)S(1)} async-done(((bf16[8,32,1024]{2,1,0:T(8,128)(2,1)}), bf16[8,32,1024]{2,1,0:T(8,128)(2,1)S(1)}, u32[]{:S(2)}, u32[]{:S(2)}) %all-to-all-start.3) | async-done | bytes 524320 | tf_op jit(solution)/shard_map/all_to_all | solution.py:34
  90.8 0.7 broadcast_in_dim.10
  91.5 4.6 %collective-permute-start.4 = (bf16[256,1024]{1,0:T(8,128)(2,1)S(1)}, bf16[256,1024]{1,0:T(8,128)(2,1)S(1)}, u32[]{:S(2)}, u32[]{:S(2)}) collective-permute-start(bf16[256,1024]{1,0:T(8,128)(2,1)S(1)} %bitcast.20), channel_id=1, source_target_pairs={{0,256},{256,0},{1,257},{257,1},{2,258},{258,2},{3,259},{259,3},{4... | collective-permute-start | bytes 1572872 | tf_op jit(solution)/shard_map/ppermute | solution.py:139
  96.1 3.4 %all-to-all-start.5 = ((bf16[8,32,512]{2,1,0:T(8,128)(2,1)}), bf16[8,32,512]{2,1,0:T(8,128)(2,1)S(1)}, u32[]{:S(2)}, u32[]{:S(2)}) async-start(bf16[8,32,512]{2,1,0:T(8,128)(2,1)} %broadcast_in_dim.10), calls=%async_computation.5 | async-start | bytes 524288 | tf_op jit(solution)/shard_map/all_to_all | solution.py:34
  99.6 0.0 copy-start.2
  99.6 1.8 %fusion.9 = f32[256,512]{1,0:T(8,128)S(1)} fusion(bf16[256,1024]{1,0:T(8,128)(2,1)S(1)} %bitcast.21, bf16[512,1024]{1,0:T(8,128)(2,1)} %pad_maximum_fusion), kind=kOutput, calls=%fused_computation.40 | convolution fusion | flops 268435456 | bytes 2097152 | tf_op jit(solution)/shard_map/dot_general | solution.py:25
  101.4 5.1 %collective-permute-done.4.far_gu = bf16[256,1024]{1,0:T(8,128)(2,1)S(1)} collective-permute-done((bf16[256,1024]{1,0:T(8,128)(2,1)S(1)}, bf16[256,1024]{1,0:T(8,128)(2,1)S(1)}, u32[]{:S(2)}, u32[]{:S(2)}) %collective-permute-start.4) | collective-permute-done | bytes 524320 | tf_op jit(solution)/shard_map/ppermute | solution.py:139
  106.5 0.0 copy-done.2
  106.5 1.2 fusion
  107.7 0.0 all-to-all-done.5
  107.7 8.6 %all-to-all-start.4 = ((bf16[16,16,512]{2,1,0:T(8,128)(2,1)}), bf16[16,16,512]{2,1,0:T(8,128)(2,1)}, u32[]{:S(2)}, u32[]{:S(2)}) async-start(bf16[16,16,512]{2,1,0:T(8,128)(2,1)} %bitcast.27), calls=%async_computation.4 | async-start | bytes 524288 | tf_op jit(solution)/shard_map/all_to_all | solution.py:34
  116.3 4.6 %collective-permute-start.7 = (bf16[256,512]{1,0:T(8,128)(2,1)S(1)}, bf16[256,512]{1,0:T(8,128)(2,1)S(1)}, u32[]{:S(2)}, u32[]{:S(2)}) collective-permute-start(bf16[256,512]{1,0:T(8,128)(2,1)S(1)} %bitcast.24), channel_id=1, source_target_pairs={{0,256},{256,0},{1,257},{257,1},{2,258},{258,2},{3,259},{259,3},{4... | collective-permute-start | bytes 786440 | tf_op jit(solution)/shard_map/ppermute | solution.py:137
  120.9 5.3 %collective-permute-start.5 = (bf16[256,512]{1,0:T(8,128)(2,1)S(1)}, bf16[256,512]{1,0:T(8,128)(2,1)S(1)}, u32[]{:S(2)}, u32[]{:S(2)}) collective-permute-start(bf16[256,512]{1,0:T(8,128)(2,1)S(1)} %slice.54), channel_id=1, source_target_pairs={{0,1},{1,0},{2,3},{3,2},{4,5},{5,4},{6,7},{7,6},{8,9},{9,8},{10,11... | collective-permute-start | bytes 786440 | tf_op jit(solution)/shard_map/ppermute | solution.py:145
  126.2 1.9 %collective-permute-start.6 = (bf16[256,512]{1,0:T(8,128)(2,1)S(1)}, bf16[256,512]{1,0:T(8,128)(2,1)S(1)}, u32[]{:S(2)}, u32[]{:S(2)}) collective-permute-start(bf16[256,512]{1,0:T(8,128)(2,1)S(1)} %slice.55), channel_id=1, source_target_pairs={{0,1},{1,0},{2,3},{3,2},{4,5},{5,4},{6,7},{7,6},{8,9},{9,8},{10,11... | collective-permute-start | bytes 786440 | tf_op jit(solution)/shard_map/ppermute | solution.py:146
  128.1 0.0 collective-permute-done.7.far_h
  128.1 1.5 %shard_map.85 = bf16[512,512]{1,0:T(8,128)(2,1)} custom-call(s32[1]{0:T(128)} %bitcast.5.x_hi, bf16[256,1024]{1,0:T(8,128)(2,1)S(1)} %bitcast.18, bf16[256,1024]{1,0:T(8,128)(2,1)S(1)} %collective-permute-done.2.other, bf16[256,512]{1,0:T(8,128)(2,1)S(1)} %bitcast.25, bf16[256,512]{1,0:T(8,128)(2,1)S(1)} %collective-permute-done.7.far_h), custom_call_target="tpu_custom_call" | custom-call | flops 268435456 | bytes 2097152 | tf_op jit(solution)/shard_map/pallas_call | solution.py:88
  129.6 0.0 collective-permute-done.5.other_own
  129.6 0.0 collective-permute-done.6.other_far
  129.6 1.8 %shard_map.84 = (bf16[512,512]{1,0:T(8,128)(2,1)}, bf16[512,512]{1,0:T(8,128)(2,1)}) custom-call(s32[1]{0:T(128)} %bitcast.5.x_hi, bf16[256,1024]{1,0:T(8,128)(2,1)S(1)} %bitcast.19, bf16[256,1024]{1,0:T(8,128)(2,1)S(1)} %collective-permute-done.2.other, bf16[256,1024]{1,0:T(8,128)(2,1)S(1)} %bitcast.23, ...), custom_call_target="tpu_custom_call" | custom-call | flops 536870912 | bytes 4194304 | tf_op jit(solution)/shard_map/pallas_call | solution.py:62
  131.4 0.0 all-to-all-done.4
  131.4 1.6 %reduce_sum.32 = bf16[16,512]{1,0:T(8,128)(2,1)} reduce(bf16[16,16,512]{2,1,0:T(8,128)(2,1)} %all-to-all-done.4, bf16[]{:T(256)} %constant.23.clone.1), dimensions={0}, to_apply=%region_2.0 | reduce | flops 122880 | bytes 278530 | tf_op jit(solution)/shard_map/reduce_sum | solution.py:45
  (10 shorter events, 0.1 us)
Async XLA Ops:
  0.6 21.8 %copy-start = (bf16[1024,512]{1,0:T(8,128)(2,1)S(1)}, bf16[1024,512]{1,0:T(8,128)(2,1)}, u32[]{:S(2)}) copy-start(bf16[1024,512]{1,0:T(8,128)(2,1)} %param.9) | copy-start | bytes 3145732
  0.6 11.0 %copy-start.4 = (bf16[512,1024]{1,0:T(8,128)(2,1)S(1)}, bf16[512,1024]{1,0:T(8,128)(2,1)}, u32[]{:S(2)}) copy-start(bf16[512,1024]{1,0:T(8,128)(2,1)} %param.8) | copy-start | bytes 3145732
  2.4 20.0 %all-to-all-start = ((bf16[16,16,1024]{2,1,0:T(8,128)(2,1)}), bf16[16,16,1024]{2,1,0:T(8,128)(2,1)S(1)}, u32[]{:S(2)}, u32[]{:S(2)}) async-start(bf16[16,16,1024]{2,1,0:T(8,128)(2,1)} %broadcast_in_dim.8), calls=%async_computation | async-start | bytes 1048576 | tf_op jit(solution)/shard_map/all_to_all | solution.py:34
  14.3 22.0 %copy-start.1 = (bf16[512,1024]{1,0:T(8,128)(2,1)}, bf16[512,1024]{1,0:T(8,128)(2,1)S(1)}, u32[]{:S(2)}) copy-start(bf16[512,1024]{1,0:T(8,128)(2,1)S(1)} %pad_maximum_fusion.1) | copy-start | bytes 3145732
  23.7 28.9 %all-to-all-start.1 = ((bf16[8,32,1024]{2,1,0:T(8,128)(2,1)}), bf16[8,32,1024]{2,1,0:T(8,128)(2,1)S(1)}, u32[]{:S(2)}, u32[]{:S(2)}) async-start(bf16[8,32,1024]{2,1,0:T(8,128)(2,1)} %bitcast.1), calls=%async_computation.1 | async-start | bytes 1048576 | tf_op jit(solution)/shard_map/all_to_all | solution.py:34
  36.4 9.3 %copy-start.3 = (bf16[512,1024]{1,0:T(8,128)(2,1)S(1)}, bf16[512,1024]{1,0:T(8,128)(2,1)}, u32[]{:S(2)}) copy-start(bf16[512,1024]{1,0:T(8,128)(2,1)} %pad_maximum_fusion) | copy-start | bytes 3145732
  36.8 14.8 %collective-permute-start.1 = (bf16[256,1024]{1,0:T(8,128)(2,1)S(1)}, bf16[256,1024]{1,0:T(8,128)(2,1)S(1)}, u32[]{:S(2)}, u32[]{:S(2)}) collective-permute-start(bf16[256,1024]{1,0:T(8,128)(2,1)S(1)} %convolution_convert_fusion), channel_id=1, source_target_pairs={{0,256},{256,0},{1,257},{257,1},{2,258},{258,2},{3,259},{259,3},{4... | collective-permute-start | bytes 1572872 | tf_op jit(solution)/shard_map/ppermute | solution.py:117
  41.4 10.2 %collective-permute-start.2 = (bf16[256,1024]{1,0:T(8,128)(2,1)S(1)}, bf16[256,1024]{1,0:T(8,128)(2,1)S(1)}, u32[]{:S(2)}, u32[]{:S(2)}) collective-permute-start(bf16[256,1024]{1,0:T(8,128)(2,1)S(1)} %bitcast.16), channel_id=1, source_target_pairs={{0,1},{1,0},{2,3},{3,2},{4,5},{5,4},{6,7},{7,6},{8,9},{9,8},{10,11... | collective-permute-start | bytes 1572872 | tf_op jit(solution)/shard_map/ppermute | solution.py:124
  52.6 20.1 %all-to-all-start.2 = ((bf16[8,32,1024]{2,1,0:T(8,128)(2,1)}), bf16[8,32,1024]{2,1,0:T(8,128)(2,1)S(1)}, u32[]{:S(2)}, u32[]{:S(2)}) async-start(bf16[8,32,1024]{2,1,0:T(8,128)(2,1)} %bitcast.26), calls=%async_computation.2 | async-start | bytes 1048576 | tf_op jit(solution)/shard_map/all_to_all | solution.py:34
  59.1 13.7 %collective-permute-start = (f32[32,512]{1,0:T(8,128)S(1)}, f32[32,512]{1,0:T(8,128)S(1)}, u32[]{:S(2)}, u32[]{:S(2)}) collective-permute-start(f32[32,512]{1,0:T(8,128)S(1)} %pad_maximum_fusion.2), channel_id=1, source_target_pairs={{0,256},{256,0},{1,257},{257,1},{2,258},{258,2},{3,259},{259,3},{4... | collective-permute-start | bytes 196616 | tf_op jit(solution)/shard_map/ppermute | solution.py:123
  73.7 17.1 %all-to-all-start.3 = ((bf16[8,32,1024]{2,1,0:T(8,128)(2,1)}), bf16[8,32,1024]{2,1,0:T(8,128)(2,1)S(1)}, u32[]{:S(2)}, u32[]{:S(2)}) async-start(bf16[8,32,1024]{2,1,0:T(8,128)(2,1)} %broadcast_in_dim.9), calls=%async_computation.3 | async-start | bytes 1048576 | tf_op jit(solution)/shard_map/all_to_all | solution.py:34
  77.2 5.9 %collective-permute-start.3 = (bf16[32,256]{1,0:T(8,128)(2,1)S(1)}, bf16[32,256]{1,0:T(8,128)(2,1)S(1)}, u32[]{:S(2)}, u32[]{:S(2)}) collective-permute-start(bf16[32,256]{1,0:T(8,128)(2,1)S(1)} %get-tuple-element.48), channel_id=1, source_target_pairs={{0,1},{1,0},{2,3},{3,2},{4,5},{5,4},{6,7},{7,6},{8,9},{9,8},{10,11... | collective-permute-start | bytes 49160 | tf_op jit(solution)/shard_map/ppermute | solution.py:133
  91.5 15.0 %collective-permute-start.4 = (bf16[256,1024]{1,0:T(8,128)(2,1)S(1)}, bf16[256,1024]{1,0:T(8,128)(2,1)S(1)}, u32[]{:S(2)}, u32[]{:S(2)}) collective-permute-start(bf16[256,1024]{1,0:T(8,128)(2,1)S(1)} %bitcast.20), channel_id=1, source_target_pairs={{0,256},{256,0},{1,257},{257,1},{2,258},{258,2},{3,259},{259,3},{4... | collective-permute-start | bytes 1572872 | tf_op jit(solution)/shard_map/ppermute | solution.py:139
  96.1 11.6 %all-to-all-start.5 = ((bf16[8,32,512]{2,1,0:T(8,128)(2,1)}), bf16[8,32,512]{2,1,0:T(8,128)(2,1)S(1)}, u32[]{:S(2)}, u32[]{:S(2)}) async-start(bf16[8,32,512]{2,1,0:T(8,128)(2,1)} %broadcast_in_dim.10), calls=%async_computation.5 | async-start | bytes 524288 | tf_op jit(solution)/shard_map/all_to_all | solution.py:34
  99.6 6.9 %copy-start.2 = (bf16[512,1024]{1,0:T(8,128)(2,1)S(1)}, bf16[512,1024]{1,0:T(8,128)(2,1)}, u32[]{:S(2)}) copy-start(bf16[512,1024]{1,0:T(8,128)(2,1)} %copy-done.1) | copy-start | bytes 3145732
  107.7 23.7 %all-to-all-start.4 = ((bf16[16,16,512]{2,1,0:T(8,128)(2,1)}), bf16[16,16,512]{2,1,0:T(8,128)(2,1)}, u32[]{:S(2)}, u32[]{:S(2)}) async-start(bf16[16,16,512]{2,1,0:T(8,128)(2,1)} %bitcast.27), calls=%async_computation.4 | async-start | bytes 524288 | tf_op jit(solution)/shard_map/all_to_all | solution.py:34
  116.3 11.9 %collective-permute-start.7 = (bf16[256,512]{1,0:T(8,128)(2,1)S(1)}, bf16[256,512]{1,0:T(8,128)(2,1)S(1)}, u32[]{:S(2)}, u32[]{:S(2)}) collective-permute-start(bf16[256,512]{1,0:T(8,128)(2,1)S(1)} %bitcast.24), channel_id=1, source_target_pairs={{0,256},{256,0},{1,257},{257,1},{2,258},{258,2},{3,259},{259,3},{4... | collective-permute-start | bytes 786440 | tf_op jit(solution)/shard_map/ppermute | solution.py:137
  120.9 8.7 %collective-permute-start.5 = (bf16[256,512]{1,0:T(8,128)(2,1)S(1)}, bf16[256,512]{1,0:T(8,128)(2,1)S(1)}, u32[]{:S(2)}, u32[]{:S(2)}) collective-permute-start(bf16[256,512]{1,0:T(8,128)(2,1)S(1)} %slice.54), channel_id=1, source_target_pairs={{0,1},{1,0},{2,3},{3,2},{4,5},{5,4},{6,7},{7,6},{8,9},{9,8},{10,11... | collective-permute-start | bytes 786440 | tf_op jit(solution)/shard_map/ppermute | solution.py:145
  126.2 3.4 %collective-permute-start.6 = (bf16[256,512]{1,0:T(8,128)(2,1)S(1)}, bf16[256,512]{1,0:T(8,128)(2,1)S(1)}, u32[]{:S(2)}, u32[]{:S(2)}) collective-permute-start(bf16[256,512]{1,0:T(8,128)(2,1)S(1)} %slice.55), channel_id=1, source_target_pairs={{0,1},{1,0},{2,3},{3,2},{4,5},{5,4},{6,7},{7,6},{8,9},{9,8},{10,11... | collective-permute-start | bytes 786440 | tf_op jit(solution)/shard_map/ppermute | solution.py:146

commit v4 on v3

--- a/solution.py
+++ b/solution.py
@@ -26,7 +26,7 @@
 
 
 Z_ORDER = (0, 4, 7, 3, 1, 5, 6, 2)
-COL_ORDER = (7, 0, 6, 2, 14, 12, 15, 8, 13, 4, 1, 9, 3, 11, 10, 5)
+COL_ORDER = (15, 1, 0, 4, 6, 5, 11, 3, 12, 13, 2, 7, 14, 10, 8, 9)
 
 
 def exchange(x, axis):
@@ -45,58 +45,38 @@
     return jnp.sum(exchange(x.reshape(n, rows // n, cols), axis).astype(f32), axis=0)
 
 
-def gate_up_grads_kernel(x_hi, own, other, own_gu, far_gu, other_own, other_far, gate_ref, up_ref):
-    def part(mine, others):
-        total = dot(own[...], mine[:, :512], FIRST) + dot(other[...], others[...], FIRST)
+def weight_grads_kernel(
+    x_hi, own, other, own_gu, far_gu, other_own, other_far, own_h, far_h,
+    gate_ref, up_ref, down_ref,
+):
+    def part(mine, others, h):
+        total = dot(own[:, :512], mine[:, :512], FIRST) + dot(other[:, :512], others[...], FIRST)
         gate_ref[...] = total[:, :256].astype(bf16)
         up_ref[...] = total[:, 256:].astype(bf16)
+        total = dot(h[:, :256], own[:, 512:], FIRST) + dot(h[:, 256:], other[:, 512:], FIRST)
+        down_ref[...] = total.astype(bf16)
 
-    pl.when(pl.program_id(0) == 0)(lambda: part(own_gu, other_own))
-    pl.when(pl.program_id(0) == 1)(lambda: part(far_gu, other_far))
+    pl.when(pl.program_id(0) == 0)(lambda: part(own_gu, other_own, own_h))
+    pl.when(pl.program_id(0) == 1)(lambda: part(far_gu, other_far, far_h))
 
 
-def gate_up_grads(x_hi, own, other, own_gu, far_gu, other_own, other_far):
-    whole = lambda shape: pl.BlockSpec(shape, lambda q, at: (0, 0))
-    out = pl.BlockSpec((512, 256), lambda q, at: (0, at[0] ^ q))
-    shape = jax.ShapeDtypeStruct((512, 512), bf16)
+def weight_grads(*args):
+    whole = lambda x: pl.BlockSpec(x.shape, lambda q, at: (0,) * x.ndim)
+    columns = pl.BlockSpec((512, 256), lambda q, at: (0, at[0] ^ q))
+    rows = pl.BlockSpec((256, 512), lambda q, at: (at[0] ^ q, 0))
+    weight = jax.ShapeDtypeStruct((512, 512), bf16)
     return pl.pallas_call(
-        gate_up_grads_kernel,
-        out_shape=(shape, shape),
+        weight_grads_kernel,
+        out_shape=(weight, weight, weight),
         grid_spec=pltpu.PrefetchScalarGridSpec(
             num_scalar_prefetch=1,
             grid=(2,),
-            in_specs=[whole((256, 512)), whole((256, 512)), whole((256, 1024)), whole((256, 1024)),
-                      whole((256, 512)), whole((256, 512))],
-            out_specs=(out, out),
+            in_specs=[whole(x) for x in args[1:]],
+            out_specs=(columns, columns, rows),
         ),
         compiler_params=pltpu.CompilerParams(vmem_limit_bytes=24 * 2**20),
-        cost_estimate=pl.CostEstimate(flops=2 * 512**3 * 2, bytes_accessed=4 * 2**20, transcendentals=0),
-    )(x_hi, own, other, own_gu, far_gu, other_own, other_far)
-
-
-def down_grads_kernel(x_hi, own, other, own_h, far_h, out_ref):
-    def part(h):
-        total = dot(h[:, :256], own[...], FIRST) + dot(h[:, 256:], other[...], FIRST)
-        out_ref[...] = total.astype(bf16)
-
-    pl.when(pl.program_id(0) == 0)(lambda: part(own_h))
-    pl.when(pl.program_id(0) == 1)(lambda: part(far_h))
-
-
-def down_grads(x_hi, own, other, own_h, far_h):
-    half = lambda column: pl.BlockSpec((256, 512), lambda q, at: (0, column))
-    return pl.pallas_call(
-        down_grads_kernel,
-        out_shape=jax.ShapeDtypeStruct((512, 512), bf16),
-        grid_spec=pltpu.PrefetchScalarGridSpec(
-            num_scalar_prefetch=1,
-            grid=(2,),
-            in_specs=[half(1), half(1), half(0), half(0)],
-            out_specs=pl.BlockSpec((256, 512), lambda q, at: (at[0] ^ q, 0)),
-        ),
-        compiler_params=pltpu.CompilerParams(vmem_limit_bytes=24 * 2**20),
-        cost_estimate=pl.CostEstimate(flops=2 * 512**3, bytes_accessed=2 * 2**20, transcendentals=0),
-    )(x_hi, own, other, own_h, far_h)
+        cost_estimate=pl.CostEstimate(flops=6 * 512**3, bytes_accessed=5 * 2**20, transcendentals=0),
+    )(*args)
 
 
 def body(tokens, grad_out, gate_weight, up_weight, down_weight):
@@ -145,10 +125,9 @@
     other_own = lax.ppermute(own_gu[:, 512:], "dp", SWAP)
     other_far = lax.ppermute(far_gu[:, 512:], "dp", SWAP)
     at = x_hi.astype(jnp.int32)[None]
-    grad_gate, grad_up = gate_up_grads(
-        at, own, other, own_gu, far_gu, other_own, other_far
+    grad_gate, grad_up, grad_down = weight_grads(
+        at, own, other, own_gu, far_gu, other_own, other_far, own_h, far_h
     )
-    grad_down = down_grads(at, own, other, own_h, far_h)
     return grad_tokens, grad_gate, grad_up, grad_down
 
 

time: 134 us -> 133 us (level)
  waiting for transfers between devices: 36.3 us -> 38.1 us
  starting transfers between devices: 78.6 us -> 76.8 us
    all_to_all x6, starting transfers between devices: 43.7 us -> 41.6 us  [exchange(): lax.all_to_all(x, axis, 0, 0, tiled=True, axis_index_groups=[list(order)])]
    ppermute x1, waiting for transfers between devices: 0.04 us -> 1.48 us  [body(): other_far = lax.ppermute(far_gu[:, 512:], 'dp', SWAP)]
    pallas_call x2 -> x1, Pallas kernels: 3.25 us -> 2.14 us  [weight_grads(): pl.pallas_call(weight_grads_kernel, out_shape=(weight, weight, weight), g...]
  transfers between devices with their start and end apart: 14 -> 14, of which waited for: 6 -> 7; matrix products, arithmetic and copies ran while one was open for 6% -> 6% of each run, Pallas kernels for 2% -> 2%
where the time goes in v4:
time: 133 us; the launch traced here: 132 us
  starting transfers between devices  76.8 us (58%)
  waiting for transfers between devices  38.1 us (29%)
  matrix products  5.11 us (4%)
  other arithmetic  4.92 us (4%)
  local copies, waits for them, and re-layouts  3.95 us (3%)
  Pallas kernels  2.14 us (2%)
    all_to_all x6, starting transfers between devices, exchange(): lax.all_to_all(x, axis, 0, 0, tiled=True, axis_index_groups=[list(order)])  41.6 us
    all_to_all x6, waiting for transfers between devices, exchange(): lax.all_to_all(x, axis, 0, 0, tiled=True, axis_index_groups=[list(order)])  25.7 us
    ppermute x1, starting transfers between devices, body(): other_own = lax.ppermute(own_gu[:, 512:], 'dp', SWAP)  5.35 us
    ppermute x1, waiting for transfers between devices, body(): far_gu = lax.ppermute(own_gu, 'x_hi', SWAP)  5.26 us
    dot_general x5, matrix products, dot(): return lax.dot_general(a, b, dims, preferred_element_type=f32)  5.11 us
    ppermute x1, starting transfers between devices, body(): lax.ppermute(hidden[:, 256:], 'dp', SWAP)  4.92 us
    ppermute x1, waiting for transfers between devices, body(): got = lax.ppermute(dot(own_in, gu_send, PLAIN).astype(bf16), 'x_hi', SWAP)  4.81 us
    ppermute x1, starting transfers between devices, body(): got = lax.ppermute(dot(own_in, gu_send, PLAIN).astype(bf16), 'x_hi', SWAP)  4.62 us
  transfers between devices with their start and end apart: 14, of which 7 were waited for; matrix products, arithmetic and copies ran while one was open for 6% of the time, Pallas kernels for 2%

profile of v4, /device:TPU:1, one launch (start us, length us, event | category | flops | bytes accessed | tf_op | source)
XLA Modules:
  0.0 131.9 jit_solution(14231576610911773427)
XLA Ops:
  0.6 0.0 copy-start
  0.6 0.0 copy-start.4
  0.7 0.9 pad_maximum_fusion.6
  1.5 0.9 broadcast_in_dim.8
  2.4 8.9 %all-to-all-start = ((bf16[16,16,1024]{2,1,0:T(8,128)(2,1)}), bf16[16,16,1024]{2,1,0:T(8,128)(2,1)S(1)}, u32[]{:S(2)}, u32[]{:S(2)}) async-start(bf16[16,16,1024]{2,1,0:T(8,128)(2,1)} %broadcast_in_dim.8), calls=%async_computation | async-start | bytes 1048576 | tf_op jit(solution)/shard_map/all_to_all | solution.py:34
  11.3 0.0 copy-done.4
  11.3 1.4 %constant_dynamic-slice_fusion.6 = (bf16[512,256]{1,0:T(8,128)(2,1)S(1)}, bf16[512,256]{1,0:T(8,128)(2,1)S(1)}, bf16[512,256]{1,0:T(8,128)(2,1)S(1)}, bf16[512,2...) fusion(bf16[512,1024]{1,0:T(8,128)(2,1)S(1)} %copy-done.4, ...), kind=kLoop, calls=%fused_computation.30 | loop fusion | bytes 4194320 | tf_op jit(solution)/shard_map/dynamic_slice | solution.py:85
  12.7 1.1 pad_maximum_fusion
  13.8 0.1 pad_maximum_fusion.1
  14.0 0.0 copy-start.1
  14.0 8.7 %all-to-all-done = bf16[16,16,1024]{2,1,0:T(8,128)(2,1)S(1)} async-done(((bf16[16,16,1024]{2,1,0:T(8,128)(2,1)}), bf16[16,16,1024]{2,1,0:T(8,128)(2,1)S(1)}, u32[]{:S(2)}, u32[]{:S(2)}) %all-to-all-start) | async-done | bytes 524320 | tf_op jit(solution)/shard_map/all_to_all | solution.py:34
  22.6 0.0 copy-done
  22.6 1.3 convolution_convert_fusion.1
  23.9 11.9 %all-to-all-start.1 = ((bf16[8,32,1024]{2,1,0:T(8,128)(2,1)}), bf16[8,32,1024]{2,1,0:T(8,128)(2,1)S(1)}, u32[]{:S(2)}, u32[]{:S(2)}) async-start(bf16[8,32,1024]{2,1,0:T(8,128)(2,1)} %bitcast.1), calls=%async_computation.1 | async-start | bytes 1048576 | tf_op jit(solution)/shard_map/all_to_all | solution.py:34
  35.8 0.0 copy-done.1
  35.9 0.0 copy-start.3
  35.9 0.4 convolution_convert_fusion
  36.3 4.6 %collective-permute-start.1 = (bf16[256,1024]{1,0:T(8,128)(2,1)S(1)}, bf16[256,1024]{1,0:T(8,128)(2,1)S(1)}, u32[]{:S(2)}, u32[]{:S(2)}) collective-permute-start(bf16[256,1024]{1,0:T(8,128)(2,1)S(1)} %convolution_convert_fusion), channel_id=1, source_target_pairs={{0,256},{256,0},{1,257},{257,1},{2,258},{258,2},{3,259},{259,3},{4... | collective-permute-start | bytes 1572872 | tf_op jit(solution)/shard_map/ppermute | solution.py:97
  40.9 4.6 %collective-permute-start.2 = (bf16[256,1024]{1,0:T(8,128)(2,1)S(1)}, bf16[256,1024]{1,0:T(8,128)(2,1)S(1)}, u32[]{:S(2)}, u32[]{:S(2)}) collective-permute-start(bf16[256,1024]{1,0:T(8,128)(2,1)S(1)} %bitcast.16), channel_id=1, source_target_pairs={{0,1},{1,0},{2,3},{3,2},{4,5},{5,4},{6,7},{7,6},{8,9},{9,8},{10,11... | collective-permute-start | bytes 1572872 | tf_op jit(solution)/shard_map/ppermute | solution.py:104
  45.5 0.0 copy-done.3
  45.5 0.4 fusion.3
  46.0 4.8 %collective-permute-done.1 = bf16[256,1024]{1,0:T(8,128)(2,1)S(1)} collective-permute-done((bf16[256,1024]{1,0:T(8,128)(2,1)S(1)}, bf16[256,1024]{1,0:T(8,128)(2,1)S(1)}, u32[]{:S(2)}, u32[]{:S(2)}) %collective-permute-start.1) | collective-permute-done | bytes 524320 | tf_op jit(solution)/shard_map/ppermute | solution.py:97
  50.8 0.0 collective-permute-done.2.other
  50.8 0.9 add_convert_fusion
  51.7 0.0 all-to-all-done.1
  51.7 6.4 %all-to-all-start.2 = ((bf16[8,32,1024]{2,1,0:T(8,128)(2,1)}), bf16[8,32,1024]{2,1,0:T(8,128)(2,1)S(1)}, u32[]{:S(2)}, u32[]{:S(2)}) async-start(bf16[8,32,1024]{2,1,0:T(8,128)(2,1)} %bitcast.25), calls=%async_computation.2 | async-start | bytes 1048576 | tf_op jit(solution)/shard_map/all_to_all | solution.py:34
  58.1 0.1 convert_reduce_fusion.1
  58.2 4.6 %collective-permute-start = (f32[32,512]{1,0:T(8,128)S(1)}, f32[32,512]{1,0:T(8,128)S(1)}, u32[]{:S(2)}, u32[]{:S(2)}) collective-permute-start(f32[32,512]{1,0:T(8,128)S(1)} %pad_maximum_fusion.2), channel_id=1, source_target_pairs={{0,256},{256,0},{1,257},{257,1},{2,258},{258,2},{3,259},{259,3},{4... | collective-permute-start | bytes 196616 | tf_op jit(solution)/shard_map/ppermute | solution.py:103
  62.8 9.1 %all-to-all-done.2 = bf16[8,32,1024]{2,1,0:T(8,128)(2,1)S(1)} async-done(((bf16[8,32,1024]{2,1,0:T(8,128)(2,1)}), bf16[8,32,1024]{2,1,0:T(8,128)(2,1)S(1)}, u32[]{:S(2)}, u32[]{:S(2)}) %all-to-all-start.2) | async-done | bytes 524320 | tf_op jit(solution)/shard_map/all_to_all | solution.py:34
  71.9 0.1 convert_reduce_fusion
  72.0 0.0 collective-permute-done
  72.0 0.1 multiply_convert_fusion.2
  72.1 0.9 broadcast_in_dim.9
  73.0 3.5 %all-to-all-start.3 = ((bf16[8,32,1024]{2,1,0:T(8,128)(2,1)}), bf16[8,32,1024]{2,1,0:T(8,128)(2,1)S(1)}, u32[]{:S(2)}, u32[]{:S(2)}) async-start(bf16[8,32,1024]{2,1,0:T(8,128)(2,1)} %broadcast_in_dim.9), calls=%async_computation.3 | async-start | bytes 1048576 | tf_op jit(solution)/shard_map/all_to_all | solution.py:34
  76.5 4.9 %collective-permute-start.3 = (bf16[32,256]{1,0:T(8,128)(2,1)S(1)}, bf16[32,256]{1,0:T(8,128)(2,1)S(1)}, u32[]{:S(2)}, u32[]{:S(2)}) collective-permute-start(bf16[32,256]{1,0:T(8,128)(2,1)S(1)} %get-tuple-element.50), channel_id=1, source_target_pairs={{0,1},{1,0},{2,3},{3,2},{4,5},{5,4},{6,7},{7,6},{8,9},{9,8},{10,11... | collective-permute-start | bytes 49160 | tf_op jit(solution)/shard_map/ppermute | solution.py:113
  81.4 0.8 collective-permute-done.3
  82.2 7.9 %all-to-all-done.3 = bf16[8,32,1024]{2,1,0:T(8,128)(2,1)S(1)} async-done(((bf16[8,32,1024]{2,1,0:T(8,128)(2,1)}), bf16[8,32,1024]{2,1,0:T(8,128)(2,1)S(1)}, u32[]{:S(2)}, u32[]{:S(2)}) %all-to-all-start.3) | async-done | bytes 524320 | tf_op jit(solution)/shard_map/all_to_all | solution.py:34
  90.2 0.7 broadcast_in_dim.10
  90.9 4.6 %collective-permute-start.4 = (bf16[256,1024]{1,0:T(8,128)(2,1)S(1)}, bf16[256,1024]{1,0:T(8,128)(2,1)S(1)}, u32[]{:S(2)}, u32[]{:S(2)}) collective-permute-start(bf16[256,1024]{1,0:T(8,128)(2,1)S(1)} %bitcast.19), channel_id=1, source_target_pairs={{0,256},{256,0},{1,257},{257,1},{2,258},{258,2},{3,259},{259,3},{4... | collective-permute-start | bytes 1572872 | tf_op jit(solution)/shard_map/ppermute | solution.py:119
  95.5 3.4 %all-to-all-start.5 = ((bf16[8,32,512]{2,1,0:T(8,128)(2,1)}), bf16[8,32,512]{2,1,0:T(8,128)(2,1)S(1)}, u32[]{:S(2)}, u32[]{:S(2)}) async-start(bf16[8,32,512]{2,1,0:T(8,128)(2,1)} %broadcast_in_dim.10), calls=%async_computation.5 | async-start | bytes 524288 | tf_op jit(solution)/shard_map/all_to_all | solution.py:34
  99.0 0.0 copy-start.2
  99.0 1.8 %fusion.9 = f32[256,512]{1,0:T(8,128)S(1)} fusion(bf16[256,1024]{1,0:T(8,128)(2,1)S(1)} %bitcast.20, bf16[512,1024]{1,0:T(8,128)(2,1)} %pad_maximum_fusion), kind=kOutput, calls=%fused_computation.40 | convolution fusion | flops 268435456 | bytes 2097152 | tf_op jit(solution)/shard_map/dot_general | solution.py:25
  100.8 5.3 %collective-permute-done.4.far_gu = bf16[256,1024]{1,0:T(8,128)(2,1)S(1)} collective-permute-done((bf16[256,1024]{1,0:T(8,128)(2,1)S(1)}, bf16[256,1024]{1,0:T(8,128)(2,1)S(1)}, u32[]{:S(2)}, u32[]{:S(2)}) %collective-permute-start.4) | collective-permute-done | bytes 524320 | tf_op jit(solution)/shard_map/ppermute | solution.py:119
  106.0 0.0 copy-done.2
  106.0 1.2 fusion
  107.2 0.0 all-to-all-done.5
  107.2 7.5 %all-to-all-start.4 = ((bf16[16,16,512]{2,1,0:T(8,128)(2,1)}), bf16[16,16,512]{2,1,0:T(8,128)(2,1)}, u32[]{:S(2)}, u32[]{:S(2)}) async-start(bf16[16,16,512]{2,1,0:T(8,128)(2,1)} %bitcast.26), calls=%async_computation.4 | async-start | bytes 524288 | tf_op jit(solution)/shard_map/all_to_all | solution.py:34
  114.7 4.6 %collective-permute-start.7 = (bf16[256,512]{1,0:T(8,128)(2,1)S(1)}, bf16[256,512]{1,0:T(8,128)(2,1)S(1)}, u32[]{:S(2)}, u32[]{:S(2)}) collective-permute-start(bf16[256,512]{1,0:T(8,128)(2,1)S(1)} %bitcast.23), channel_id=1, source_target_pairs={{0,256},{256,0},{1,257},{257,1},{2,258},{258,2},{3,259},{259,3},{4... | collective-permute-start | bytes 786440 | tf_op jit(solution)/shard_map/ppermute | solution.py:117
  119.4 5.3 %collective-permute-start.5 = (bf16[256,512]{1,0:T(8,128)(2,1)S(1)}, bf16[256,512]{1,0:T(8,128)(2,1)S(1)}, u32[]{:S(2)}, u32[]{:S(2)}) collective-permute-start(bf16[256,512]{1,0:T(8,128)(2,1)S(1)} %slice.54), channel_id=1, source_target_pairs={{0,1},{1,0},{2,3},{3,2},{4,5},{5,4},{6,7},{7,6},{8,9},{9,8},{10,11... | collective-permute-start | bytes 786440 | tf_op jit(solution)/shard_map/ppermute | solution.py:125
  124.7 1.9 %collective-permute-start.6 = (bf16[256,512]{1,0:T(8,128)(2,1)S(1)}, bf16[256,512]{1,0:T(8,128)(2,1)S(1)}, u32[]{:S(2)}, u32[]{:S(2)}) collective-permute-start(bf16[256,512]{1,0:T(8,128)(2,1)S(1)} %slice.55), channel_id=1, source_target_pairs={{0,1},{1,0},{2,3},{3,2},{4,5},{5,4},{6,7},{7,6},{8,9},{9,8},{10,11... | collective-permute-start | bytes 786440 | tf_op jit(solution)/shard_map/ppermute | solution.py:126
  126.7 0.0 collective-permute-done.7.far_h
  126.7 0.0 collective-permute-done.5.other_own
  126.7 1.5 %collective-permute-done.6.other_far = bf16[256,512]{1,0:T(8,128)(2,1)S(1)} collective-permute-done((bf16[256,512]{1,0:T(8,128)(2,1)S(1)}, bf16[256,512]{1,0:T(8,128)(2,1)S(1)}, u32[]{:S(2)}, u32[]{:S(2)}) %collective-permute-start.6) | collective-permute-done | bytes 262176 | tf_op jit(solution)/shard_map/ppermute | solution.py:126
  128.2 2.1 %shard_map.84 = (bf16[512,512]{1,0:T(8,128)(2,1)}, bf16[512,512]{1,0:T(8,128)(2,1)}, bf16[512,512]{1,0:T(8,128)(2,1)}) custom-call(s32[1]{0:T(128)} %bitcast.5.x_hi, bf16[256,1024]{1,0:T(8,128)(2,1)S(1)} %bitcast.18, bf16[256,1024]{1,0:T(8,128)(2,1)S(1)} %collective-permute-done.2.other, bf16[256,1024]{1,0:T(8,128)(2,1)S(1)} %bitcast.22, ...), custom_call_target="tpu_custom_call" | custom-call | flops 805306368 | bytes 5242880 | tf_op jit(solution)/shard_map/pallas_call | solution.py:68
  130.3 0.0 all-to-all-done.4
  130.3 1.6 %reduce_sum.32 = bf16[16,512]{1,0:T(8,128)(2,1)} reduce(bf16[16,16,512]{2,1,0:T(8,128)(2,1)} %all-to-all-done.4, bf16[]{:T(256)} %constant.23.clone.1), dimensions={0}, to_apply=%region_2.0 | reduce | flops 122880 | bytes 278530 | tf_op jit(solution)/shard_map/reduce_sum | solution.py:45
  (10 shorter events, 0.1 us)
Async XLA Ops:
  0.6 22.0 %copy-start = (bf16[1024,512]{1,0:T(8,128)(2,1)S(1)}, bf16[1024,512]{1,0:T(8,128)(2,1)}, u32[]{:S(2)}) copy-start(bf16[1024,512]{1,0:T(8,128)(2,1)} %param.9) | copy-start | bytes 3145732
  0.6 10.6 %copy-start.4 = (bf16[512,1024]{1,0:T(8,128)(2,1)S(1)}, bf16[512,1024]{1,0:T(8,128)(2,1)}, u32[]{:S(2)}) copy-start(bf16[512,1024]{1,0:T(8,128)(2,1)} %param.8) | copy-start | bytes 3145732
  2.4 20.2 %all-to-all-start = ((bf16[16,16,1024]{2,1,0:T(8,128)(2,1)}), bf16[16,16,1024]{2,1,0:T(8,128)(2,1)S(1)}, u32[]{:S(2)}, u32[]{:S(2)}) async-start(bf16[16,16,1024]{2,1,0:T(8,128)(2,1)} %broadcast_in_dim.8), calls=%async_computation | async-start | bytes 1048576 | tf_op jit(solution)/shard_map/all_to_all | solution.py:34
  14.0 21.9 %copy-start.1 = (bf16[512,1024]{1,0:T(8,128)(2,1)}, bf16[512,1024]{1,0:T(8,128)(2,1)S(1)}, u32[]{:S(2)}) copy-start(bf16[512,1024]{1,0:T(8,128)(2,1)S(1)} %pad_maximum_fusion.1) | copy-start | bytes 3145732
  23.9 27.8 %all-to-all-start.1 = ((bf16[8,32,1024]{2,1,0:T(8,128)(2,1)}), bf16[8,32,1024]{2,1,0:T(8,128)(2,1)S(1)}, u32[]{:S(2)}, u32[]{:S(2)}) async-start(bf16[8,32,1024]{2,1,0:T(8,128)(2,1)} %bitcast.1), calls=%async_computation.1 | async-start | bytes 1048576 | tf_op jit(solution)/shard_map/all_to_all | solution.py:34
  35.9 9.6 %copy-start.3 = (bf16[512,1024]{1,0:T(8,128)(2,1)S(1)}, bf16[512,1024]{1,0:T(8,128)(2,1)}, u32[]{:S(2)}) copy-start(bf16[512,1024]{1,0:T(8,128)(2,1)} %pad_maximum_fusion) | copy-start | bytes 3145732
  36.3 14.5 %collective-permute-start.1 = (bf16[256,1024]{1,0:T(8,128)(2,1)S(1)}, bf16[256,1024]{1,0:T(8,128)(2,1)S(1)}, u32[]{:S(2)}, u32[]{:S(2)}) collective-permute-start(bf16[256,1024]{1,0:T(8,128)(2,1)S(1)} %convolution_convert_fusion), channel_id=1, source_target_pairs={{0,256},{256,0},{1,257},{257,1},{2,258},{258,2},{3,259},{259,3},{4... | collective-permute-start | bytes 1572872 | tf_op jit(solution)/shard_map/ppermute | solution.py:97
  40.9 9.8 %collective-permute-start.2 = (bf16[256,1024]{1,0:T(8,128)(2,1)S(1)}, bf16[256,1024]{1,0:T(8,128)(2,1)S(1)}, u32[]{:S(2)}, u32[]{:S(2)}) collective-permute-start(bf16[256,1024]{1,0:T(8,128)(2,1)S(1)} %bitcast.16), channel_id=1, source_target_pairs={{0,1},{1,0},{2,3},{3,2},{4,5},{5,4},{6,7},{7,6},{8,9},{9,8},{10,11... | collective-permute-start | bytes 1572872 | tf_op jit(solution)/shard_map/ppermute | solution.py:104
  51.7 20.2 %all-to-all-start.2 = ((bf16[8,32,1024]{2,1,0:T(8,128)(2,1)}), bf16[8,32,1024]{2,1,0:T(8,128)(2,1)S(1)}, u32[]{:S(2)}, u32[]{:S(2)}) async-start(bf16[8,32,1024]{2,1,0:T(8,128)(2,1)} %bitcast.25), calls=%async_computation.2 | async-start | bytes 1048576 | tf_op jit(solution)/shard_map/all_to_all | solution.py:34
  58.2 13.8 %collective-permute-start = (f32[32,512]{1,0:T(8,128)S(1)}, f32[32,512]{1,0:T(8,128)S(1)}, u32[]{:S(2)}, u32[]{:S(2)}) collective-permute-start(f32[32,512]{1,0:T(8,128)S(1)} %pad_maximum_fusion.2), channel_id=1, source_target_pairs={{0,256},{256,0},{1,257},{257,1},{2,258},{258,2},{3,259},{259,3},{4... | collective-permute-start | bytes 196616 | tf_op jit(solution)/shard_map/ppermute | solution.py:103
  73.0 17.2 %all-to-all-start.3 = ((bf16[8,32,1024]{2,1,0:T(8,128)(2,1)}), bf16[8,32,1024]{2,1,0:T(8,128)(2,1)S(1)}, u32[]{:S(2)}, u32[]{:S(2)}) async-start(bf16[8,32,1024]{2,1,0:T(8,128)(2,1)} %broadcast_in_dim.9), calls=%async_computation.3 | async-start | bytes 1048576 | tf_op jit(solution)/shard_map/all_to_all | solution.py:34
  76.5 5.7 %collective-permute-start.3 = (bf16[32,256]{1,0:T(8,128)(2,1)S(1)}, bf16[32,256]{1,0:T(8,128)(2,1)S(1)}, u32[]{:S(2)}, u32[]{:S(2)}) collective-permute-start(bf16[32,256]{1,0:T(8,128)(2,1)S(1)} %get-tuple-element.50), channel_id=1, source_target_pairs={{0,1},{1,0},{2,3},{3,2},{4,5},{5,4},{6,7},{7,6},{8,9},{9,8},{10,11... | collective-permute-start | bytes 49160 | tf_op jit(solution)/shard_map/ppermute | solution.py:113
  90.9 15.1 %collective-permute-start.4 = (bf16[256,1024]{1,0:T(8,128)(2,1)S(1)}, bf16[256,1024]{1,0:T(8,128)(2,1)S(1)}, u32[]{:S(2)}, u32[]{:S(2)}) collective-permute-start(bf16[256,1024]{1,0:T(8,128)(2,1)S(1)} %bitcast.19), channel_id=1, source_target_pairs={{0,256},{256,0},{1,257},{257,1},{2,258},{258,2},{3,259},{259,3},{4... | collective-permute-start | bytes 1572872 | tf_op jit(solution)/shard_map/ppermute | solution.py:119
  95.5 11.7 %all-to-all-start.5 = ((bf16[8,32,512]{2,1,0:T(8,128)(2,1)}), bf16[8,32,512]{2,1,0:T(8,128)(2,1)S(1)}, u32[]{:S(2)}, u32[]{:S(2)}) async-start(bf16[8,32,512]{2,1,0:T(8,128)(2,1)} %broadcast_in_dim.10), calls=%async_computation.5 | async-start | bytes 524288 | tf_op jit(solution)/shard_map/all_to_all | solution.py:34
  99.0 7.1 %copy-start.2 = (bf16[512,1024]{1,0:T(8,128)(2,1)S(1)}, bf16[512,1024]{1,0:T(8,128)(2,1)}, u32[]{:S(2)}) copy-start(bf16[512,1024]{1,0:T(8,128)(2,1)} %copy-done.1) | copy-start | bytes 3145732
  107.2 23.1 %all-to-all-start.4 = ((bf16[16,16,512]{2,1,0:T(8,128)(2,1)}), bf16[16,16,512]{2,1,0:T(8,128)(2,1)}, u32[]{:S(2)}, u32[]{:S(2)}) async-start(bf16[16,16,512]{2,1,0:T(8,128)(2,1)} %bitcast.26), calls=%async_computation.4 | async-start | bytes 524288 | tf_op jit(solution)/shard_map/all_to_all | solution.py:34
  114.7 12.0 %collective-permute-start.7 = (bf16[256,512]{1,0:T(8,128)(2,1)S(1)}, bf16[256,512]{1,0:T(8,128)(2,1)S(1)}, u32[]{:S(2)}, u32[]{:S(2)}) collective-permute-start(bf16[256,512]{1,0:T(8,128)(2,1)S(1)} %bitcast.23), channel_id=1, source_target_pairs={{0,256},{256,0},{1,257},{257,1},{2,258},{258,2},{3,259},{259,3},{4... | collective-permute-start | bytes 786440 | tf_op jit(solution)/shard_map/ppermute | solution.py:117
  119.4 7.3 %collective-permute-start.5 = (bf16[256,512]{1,0:T(8,128)(2,1)S(1)}, bf16[256,512]{1,0:T(8,128)(2,1)S(1)}, u32[]{:S(2)}, u32[]{:S(2)}) collective-permute-start(bf16[256,512]{1,0:T(8,128)(2,1)S(1)} %slice.54), channel_id=1, source_target_pairs={{0,1},{1,0},{2,3},{3,2},{4,5},{5,4},{6,7},{7,6},{8,9},{9,8},{10,11... | collective-permute-start | bytes 786440 | tf_op jit(solution)/shard_map/ppermute | solution.py:125
  124.7 3.4 %collective-permute-start.6 = (bf16[256,512]{1,0:T(8,128)(2,1)S(1)}, bf16[256,512]{1,0:T(8,128)(2,1)S(1)}, u32[]{:S(2)}, u32[]{:S(2)}) collective-permute-start(bf16[256,512]{1,0:T(8,128)(2,1)S(1)} %slice.55), channel_id=1, source_target_pairs={{0,1},{1,0},{2,3},{3,2},{4,5},{5,4},{6,7},{7,6},{8,9},{9,8},{10,11... | collective-permute-start | bytes 786440 | tf_op jit(solution)/shard_map/ppermute | solution.py:126

commit v5 on v4

--- a/solution.py
+++ b/solution.py
@@ -26,7 +26,7 @@
 
 
 Z_ORDER = (0, 4, 7, 3, 1, 5, 6, 2)
-COL_ORDER = (15, 1, 0, 4, 6, 5, 11, 3, 12, 13, 2, 7, 14, 10, 8, 9)
+COL_ORDER = (0, 2, 4, 6, 8, 10, 12, 14, 1, 3, 5, 7, 9, 11, 13, 15)
 
 
 def exchange(x, axis):

time: 133 us -> 132 us (level)
  waiting for transfers between devices: 38.1 us -> 27.1 us
  starting transfers between devices: 76.8 us -> 87.1 us
    all_to_all x6, starting transfers between devices: 41.6 us -> 50 us  [exchange(): lax.all_to_all(x, axis, 0, 0, tiled=True, axis_index_groups=[list(order)])]
    ppermute x1, waiting for transfers between devices: 5.26 us -> 0.01 us  [body(): far_gu = lax.ppermute(own_gu, 'x_hi', SWAP)]
    all_to_all x6, waiting for transfers between devices: 25.7 us -> 21.3 us  [exchange(): lax.all_to_all(x, axis, 0, 0, tiled=True, axis_index_groups=[list(order)])]
    ppermute x1, starting transfers between devices: 4.92 us -> 7.38 us  [body(): lax.ppermute(hidden[:, 256:], 'dp', SWAP)]
    ppermute x1, waiting for transfers between devices: 4.81 us -> 3.43 us  [body(): got = lax.ppermute(dot(own_in, gu_send, PLAIN).astype(bf16), 'x_hi', SWAP)]
where the time goes in v5:
time: 132 us; the launch traced here: 131 us
  starting transfers between devices  87.1 us (66%)
  waiting for transfers between devices  27.1 us (21%)
  matrix products  5.12 us (4%)
  other arithmetic  4.92 us (4%)
  local copies, waits for them, and re-layouts  3.95 us (3%)
  Pallas kernels  2.14 us (2%)
    all_to_all x6, starting transfers between devices, exchange(): lax.all_to_all(x, axis, 0, 0, tiled=True, axis_index_groups=[list(order)])  50 us
    all_to_all x6, waiting for transfers between devices, exchange(): lax.all_to_all(x, axis, 0, 0, tiled=True, axis_index_groups=[list(order)])  21.3 us
    ppermute x1, starting transfers between devices, body(): lax.ppermute(hidden[:, 256:], 'dp', SWAP)  7.38 us
    ppermute x1, starting transfers between devices, body(): other = lax.ppermute(own, 'dp', SWAP)  5.37 us
    dot_general x5, matrix products, dot(): return lax.dot_general(a, b, dims, preferred_element_type=f32)  5.12 us
    ppermute x1, starting transfers between devices, body(): other_own = lax.ppermute(own_gu[:, 512:], 'dp', SWAP)  5.03 us
    ppermute x1, starting transfers between devices, body(): gh = grad_hidden(x_hi) + lax.ppermute(grad_hidden(1 - x_hi), 'x_hi', SWAP)  4.36 us
    ppermute x1, starting transfers between devices, body(): far_h = lax.ppermute(own_h, 'x_hi', SWAP)  4.36 us
  transfers between devices with their start and end apart: 14, of which 7 were waited for; matrix products, arithmetic and copies ran while one was open for 6% of the time, Pallas kernels for 2%

profile of v5, /device:TPU:1, one launch (start us, length us, event | category | flops | bytes accessed | tf_op | source)
XLA Modules:
  0.0 131.3 jit_solution(3927688258255715144)
XLA Ops:
  0.6 0.0 copy-start
  0.6 0.0 copy-start.4
  0.7 0.9 pad_maximum_fusion.6
  1.5 0.9 broadcast_in_dim.8
  2.4 8.7 %all-to-all-start = ((bf16[16,16,1024]{2,1,0:T(8,128)(2,1)}), bf16[16,16,1024]{2,1,0:T(8,128)(2,1)S(1)}, u32[]{:S(2)}, u32[]{:S(2)}) async-start(bf16[16,16,1024]{2,1,0:T(8,128)(2,1)} %broadcast_in_dim.8), calls=%async_computation | async-start | bytes 1048576 | tf_op jit(solution)/shard_map/all_to_all | solution.py:34
  11.1 0.0 copy-done.4
  11.1 1.4 %constant_dynamic-slice_fusion.6 = (bf16[512,256]{1,0:T(8,128)(2,1)S(1)}, bf16[512,256]{1,0:T(8,128)(2,1)S(1)}, bf16[512,256]{1,0:T(8,128)(2,1)S(1)}, bf16[512,2...) fusion(bf16[512,1024]{1,0:T(8,128)(2,1)S(1)} %copy-done.4, ...), kind=kLoop, calls=%fused_computation.30 | loop fusion | bytes 4194320 | tf_op jit(solution)/shard_map/dynamic_slice | solution.py:85
  12.5 1.1 pad_maximum_fusion
  13.7 0.1 pad_maximum_fusion.1
  13.8 0.0 copy-start.1
  13.8 10.5 %all-to-all-done = bf16[16,16,1024]{2,1,0:T(8,128)(2,1)S(1)} async-done(((bf16[16,16,1024]{2,1,0:T(8,128)(2,1)}), bf16[16,16,1024]{2,1,0:T(8,128)(2,1)S(1)}, u32[]{:S(2)}, u32[]{:S(2)}) %all-to-all-start) | async-done | bytes 524320 | tf_op jit(solution)/shard_map/all_to_all | solution.py:34
  24.3 0.0 copy-done
  24.3 1.3 convolution_convert_fusion.1
  25.5 10.6 %all-to-all-start.1 = ((bf16[8,32,1024]{2,1,0:T(8,128)(2,1)}), bf16[8,32,1024]{2,1,0:T(8,128)(2,1)S(1)}, u32[]{:S(2)}, u32[]{:S(2)}) async-start(bf16[8,32,1024]{2,1,0:T(8,128)(2,1)} %bitcast.1), calls=%async_computation.1 | async-start | bytes 1048576 | tf_op jit(solution)/shard_map/all_to_all | solution.py:34
  36.1 0.0 copy-done.1
  36.1 0.0 copy-start.3
  36.2 0.4 convolution_convert_fusion
  36.6 4.4 %collective-permute-start.1 = (bf16[256,1024]{1,0:T(8,128)(2,1)S(1)}, bf16[256,1024]{1,0:T(8,128)(2,1)S(1)}, u32[]{:S(2)}, u32[]{:S(2)}) collective-permute-start(bf16[256,1024]{1,0:T(8,128)(2,1)S(1)} %convolution_convert_fusion), channel_id=1, source_target_pairs={{0,256},{256,0},{1,257},{257,1},{2,258},{258,2},{3,259},{259,3},{4... | collective-permute-start | bytes 1572872 | tf_op jit(solution)/shard_map/ppermute | solution.py:97
  41.0 5.4 %collective-permute-start.2 = (bf16[256,1024]{1,0:T(8,128)(2,1)S(1)}, bf16[256,1024]{1,0:T(8,128)(2,1)S(1)}, u32[]{:S(2)}, u32[]{:S(2)}) collective-permute-start(bf16[256,1024]{1,0:T(8,128)(2,1)S(1)} %bitcast.16), channel_id=1, source_target_pairs={{0,1},{1,0},{2,3},{3,2},{4,5},{5,4},{6,7},{7,6},{8,9},{9,8},{10,11... | collective-permute-start | bytes 1572872 | tf_op jit(solution)/shard_map/ppermute | solution.py:104
  46.3 0.0 copy-done.3
  46.4 0.4 fusion.3
  46.8 3.4 %collective-permute-done.1 = bf16[256,1024]{1,0:T(8,128)(2,1)S(1)} collective-permute-done((bf16[256,1024]{1,0:T(8,128)(2,1)S(1)}, bf16[256,1024]{1,0:T(8,128)(2,1)S(1)}, u32[]{:S(2)}, u32[]{:S(2)}) %collective-permute-start.1) | collective-permute-done | bytes 524320 | tf_op jit(solution)/shard_map/ppermute | solution.py:97
  50.2 0.0 collective-permute-done.2.other
  50.2 0.9 add_convert_fusion
  51.2 0.0 all-to-all-done.1
  51.2 6.4 %all-to-all-start.2 = ((bf16[8,32,1024]{2,1,0:T(8,128)(2,1)}), bf16[8,32,1024]{2,1,0:T(8,128)(2,1)S(1)}, u32[]{:S(2)}, u32[]{:S(2)}) async-start(bf16[8,32,1024]{2,1,0:T(8,128)(2,1)} %bitcast.25), calls=%async_computation.2 | async-start | bytes 1048576 | tf_op jit(solution)/shard_map/all_to_all | solution.py:34
  57.5 0.1 convert_reduce_fusion.1
  57.7 4.4 %collective-permute-start = (f32[32,512]{1,0:T(8,128)S(1)}, f32[32,512]{1,0:T(8,128)S(1)}, u32[]{:S(2)}, u32[]{:S(2)}) collective-permute-start(f32[32,512]{1,0:T(8,128)S(1)} %pad_maximum_fusion.2), channel_id=1, source_target_pairs={{0,256},{256,0},{1,257},{257,1},{2,258},{258,2},{3,259},{259,3},{4... | collective-permute-start | bytes 196616 | tf_op jit(solution)/shard_map/ppermute | solution.py:103
  62.0 5.4 %all-to-all-done.2 = bf16[8,32,1024]{2,1,0:T(8,128)(2,1)S(1)} async-done(((bf16[8,32,1024]{2,1,0:T(8,128)(2,1)}), bf16[8,32,1024]{2,1,0:T(8,128)(2,1)S(1)}, u32[]{:S(2)}, u32[]{:S(2)}) %all-to-all-start.2) | async-done | bytes 524320 | tf_op jit(solution)/shard_map/all_to_all | solution.py:34
  67.4 0.1 convert_reduce_fusion
  67.5 0.0 collective-permute-done
  67.6 0.1 multiply_convert_fusion.2
  67.7 0.9 broadcast_in_dim.9
  68.5 5.0 %all-to-all-start.3 = ((bf16[8,32,1024]{2,1,0:T(8,128)(2,1)}), bf16[8,32,1024]{2,1,0:T(8,128)(2,1)S(1)}, u32[]{:S(2)}, u32[]{:S(2)}) async-start(bf16[8,32,1024]{2,1,0:T(8,128)(2,1)} %broadcast_in_dim.9), calls=%async_computation.3 | async-start | bytes 1048576 | tf_op jit(solution)/shard_map/all_to_all | solution.py:34
  73.5 7.4 %collective-permute-start.3 = (bf16[32,256]{1,0:T(8,128)(2,1)S(1)}, bf16[32,256]{1,0:T(8,128)(2,1)S(1)}, u32[]{:S(2)}, u32[]{:S(2)}) collective-permute-start(bf16[32,256]{1,0:T(8,128)(2,1)S(1)} %get-tuple-element.50), channel_id=1, source_target_pairs={{0,1},{1,0},{2,3},{3,2},{4,5},{5,4},{6,7},{7,6},{8,9},{9,8},{10,11... | collective-permute-start | bytes 49160 | tf_op jit(solution)/shard_map/ppermute | solution.py:113
  80.9 0.8 collective-permute-done.3
  81.7 1.0 all-to-all-done.3
  82.7 0.7 broadcast_in_dim.10
  83.4 4.3 %collective-permute-start.4 = (bf16[256,1024]{1,0:T(8,128)(2,1)S(1)}, bf16[256,1024]{1,0:T(8,128)(2,1)S(1)}, u32[]{:S(2)}, u32[]{:S(2)}) collective-permute-start(bf16[256,1024]{1,0:T(8,128)(2,1)S(1)} %bitcast.19), channel_id=1, source_target_pairs={{0,256},{256,0},{1,257},{257,1},{2,258},{258,2},{3,259},{259,3},{4... | collective-permute-start | bytes 1572872 | tf_op jit(solution)/shard_map/ppermute | solution.py:119
  87.8 6.0 %all-to-all-start.5 = ((bf16[8,32,512]{2,1,0:T(8,128)(2,1)}), bf16[8,32,512]{2,1,0:T(8,128)(2,1)S(1)}, u32[]{:S(2)}, u32[]{:S(2)}) async-start(bf16[8,32,512]{2,1,0:T(8,128)(2,1)} %broadcast_in_dim.10), calls=%async_computation.5 | async-start | bytes 524288 | tf_op jit(solution)/shard_map/all_to_all | solution.py:34
  93.7 0.0 copy-start.2
  93.7 1.8 %fusion.9 = f32[256,512]{1,0:T(8,128)S(1)} fusion(bf16[256,1024]{1,0:T(8,128)(2,1)S(1)} %bitcast.20, bf16[512,1024]{1,0:T(8,128)(2,1)} %pad_maximum_fusion), kind=kOutput, calls=%fused_computation.40 | convolution fusion | flops 268435456 | bytes 2097152 | tf_op jit(solution)/shard_map/dot_general | solution.py:25
  95.5 0.0 collective-permute-done.4.far_gu
  95.5 0.0 copy-done.2
  95.5 1.2 fusion
  96.7 4.5 %all-to-all-done.5 = bf16[8,32,512]{2,1,0:T(8,128)(2,1)S(1)} async-done(((bf16[8,32,512]{2,1,0:T(8,128)(2,1)}), bf16[8,32,512]{2,1,0:T(8,128)(2,1)S(1)}, u32[]{:S(2)}, u32[]{:S(2)}) %all-to-all-start.5) | async-done | bytes 262176 | tf_op jit(solution)/shard_map/all_to_all | solution.py:34
  101.2 13.4 %all-to-all-start.4 = ((bf16[16,16,512]{2,1,0:T(8,128)(2,1)}), bf16[16,16,512]{2,1,0:T(8,128)(2,1)}, u32[]{:S(2)}, u32[]{:S(2)}) async-start(bf16[16,16,512]{2,1,0:T(8,128)(2,1)} %bitcast.26), calls=%async_computation.4 | async-start | bytes 524288 | tf_op jit(solution)/shard_map/all_to_all | solution.py:34
  114.6 4.4 %collective-permute-start.7 = (bf16[256,512]{1,0:T(8,128)(2,1)S(1)}, bf16[256,512]{1,0:T(8,128)(2,1)S(1)}, u32[]{:S(2)}, u32[]{:S(2)}) collective-permute-start(bf16[256,512]{1,0:T(8,128)(2,1)S(1)} %bitcast.23), channel_id=1, source_target_pairs={{0,256},{256,0},{1,257},{257,1},{2,258},{258,2},{3,259},{259,3},{4... | collective-permute-start | bytes 786440 | tf_op jit(solution)/shard_map/ppermute | solution.py:117
  119.0 5.0 %collective-permute-start.5 = (bf16[256,512]{1,0:T(8,128)(2,1)S(1)}, bf16[256,512]{1,0:T(8,128)(2,1)S(1)}, u32[]{:S(2)}, u32[]{:S(2)}) collective-permute-start(bf16[256,512]{1,0:T(8,128)(2,1)S(1)} %slice.54), channel_id=1, source_target_pairs={{0,1},{1,0},{2,3},{3,2},{4,5},{5,4},{6,7},{7,6},{8,9},{9,8},{10,11... | collective-permute-start | bytes 786440 | tf_op jit(solution)/shard_map/ppermute | solution.py:125
  124.1 1.9 %collective-permute-start.6 = (bf16[256,512]{1,0:T(8,128)(2,1)S(1)}, bf16[256,512]{1,0:T(8,128)(2,1)S(1)}, u32[]{:S(2)}, u32[]{:S(2)}) collective-permute-start(bf16[256,512]{1,0:T(8,128)(2,1)S(1)} %slice.55), channel_id=1, source_target_pairs={{0,1},{1,0},{2,3},{3,2},{4,5},{5,4},{6,7},{7,6},{8,9},{9,8},{10,11... | collective-permute-start | bytes 786440 | tf_op jit(solution)/shard_map/ppermute | solution.py:126
  126.0 0.0 collective-permute-done.7.far_h
  126.0 0.0 collective-permute-done.5.other_own
  126.0 1.5 %collective-permute-done.6.other_far = bf16[256,512]{1,0:T(8,128)(2,1)S(1)} collective-permute-done((bf16[256,512]{1,0:T(8,128)(2,1)S(1)}, bf16[256,512]{1,0:T(8,128)(2,1)S(1)}, u32[]{:S(2)}, u32[]{:S(2)}) %collective-permute-start.6) | collective-permute-done | bytes 262176 | tf_op jit(solution)/shard_map/ppermute | solution.py:126
  127.5 2.1 %shard_map.84 = (bf16[512,512]{1,0:T(8,128)(2,1)}, bf16[512,512]{1,0:T(8,128)(2,1)}, bf16[512,512]{1,0:T(8,128)(2,1)}) custom-call(s32[1]{0:T(128)} %bitcast.5.x_hi, bf16[256,1024]{1,0:T(8,128)(2,1)S(1)} %bitcast.18, bf16[256,1024]{1,0:T(8,128)(2,1)S(1)} %collective-permute-done.2.other, bf16[256,1024]{1,0:T(8,128)(2,1)S(1)} %bitcast.22, ...), custom_call_target="tpu_custom_call" | custom-call | flops 805306368 | bytes 5242880 | tf_op jit(solution)/shard_map/pallas_call | solution.py:68
  129.7 0.0 all-to-all-done.4
  129.7 1.6 %reduce_sum.32 = bf16[16,512]{1,0:T(8,128)(2,1)} reduce(bf16[16,16,512]{2,1,0:T(8,128)(2,1)} %all-to-all-done.4, bf16[]{:T(256)} %constant.23.clone.1), dimensions={0}, to_apply=%region_2.0 | reduce | flops 122880 | bytes 278530 | tf_op jit(solution)/shard_map/reduce_sum | solution.py:45
  (10 shorter events, 0.1 us)
Async XLA Ops:
  0.6 23.6 %copy-start = (bf16[1024,512]{1,0:T(8,128)(2,1)S(1)}, bf16[1024,512]{1,0:T(8,128)(2,1)}, u32[]{:S(2)}) copy-start(bf16[1024,512]{1,0:T(8,128)(2,1)} %param.9) | copy-start | bytes 3145732
  0.6 10.5 %copy-start.4 = (bf16[512,1024]{1,0:T(8,128)(2,1)S(1)}, bf16[512,1024]{1,0:T(8,128)(2,1)}, u32[]{:S(2)}) copy-start(bf16[512,1024]{1,0:T(8,128)(2,1)} %param.8) | copy-start | bytes 3145732
  2.4 21.9 %all-to-all-start = ((bf16[16,16,1024]{2,1,0:T(8,128)(2,1)}), bf16[16,16,1024]{2,1,0:T(8,128)(2,1)S(1)}, u32[]{:S(2)}, u32[]{:S(2)}) async-start(bf16[16,16,1024]{2,1,0:T(8,128)(2,1)} %broadcast_in_dim.8), calls=%async_computation | async-start | bytes 1048576 | tf_op jit(solution)/shard_map/all_to_all | solution.py:34
  13.8 22.3 %copy-start.1 = (bf16[512,1024]{1,0:T(8,128)(2,1)}, bf16[512,1024]{1,0:T(8,128)(2,1)S(1)}, u32[]{:S(2)}) copy-start(bf16[512,1024]{1,0:T(8,128)(2,1)S(1)} %pad_maximum_fusion.1) | copy-start | bytes 3145732
  25.5 25.6 %all-to-all-start.1 = ((bf16[8,32,1024]{2,1,0:T(8,128)(2,1)}), bf16[8,32,1024]{2,1,0:T(8,128)(2,1)S(1)}, u32[]{:S(2)}, u32[]{:S(2)}) async-start(bf16[8,32,1024]{2,1,0:T(8,128)(2,1)} %bitcast.1), calls=%async_computation.1 | async-start | bytes 1048576 | tf_op jit(solution)/shard_map/all_to_all | solution.py:34
  36.1 10.2 %copy-start.3 = (bf16[512,1024]{1,0:T(8,128)(2,1)S(1)}, bf16[512,1024]{1,0:T(8,128)(2,1)}, u32[]{:S(2)}) copy-start(bf16[512,1024]{1,0:T(8,128)(2,1)} %pad_maximum_fusion) | copy-start | bytes 3145732
  36.6 13.6 %collective-permute-start.1 = (bf16[256,1024]{1,0:T(8,128)(2,1)S(1)}, bf16[256,1024]{1,0:T(8,128)(2,1)S(1)}, u32[]{:S(2)}, u32[]{:S(2)}) collective-permute-start(bf16[256,1024]{1,0:T(8,128)(2,1)S(1)} %convolution_convert_fusion), channel_id=1, source_target_pairs={{0,256},{256,0},{1,257},{257,1},{2,258},{258,2},{3,259},{259,3},{4... | collective-permute-start | bytes 1572872 | tf_op jit(solution)/shard_map/ppermute | solution.py:97
  41.0 9.3 %collective-permute-start.2 = (bf16[256,1024]{1,0:T(8,128)(2,1)S(1)}, bf16[256,1024]{1,0:T(8,128)(2,1)S(1)}, u32[]{:S(2)}, u32[]{:S(2)}) collective-permute-start(bf16[256,1024]{1,0:T(8,128)(2,1)S(1)} %bitcast.16), channel_id=1, source_target_pairs={{0,1},{1,0},{2,3},{3,2},{4,5},{5,4},{6,7},{7,6},{8,9},{9,8},{10,11... | collective-permute-start | bytes 1572872 | tf_op jit(solution)/shard_map/ppermute | solution.py:104
  51.2 16.3 %all-to-all-start.2 = ((bf16[8,32,1024]{2,1,0:T(8,128)(2,1)}), bf16[8,32,1024]{2,1,0:T(8,128)(2,1)S(1)}, u32[]{:S(2)}, u32[]{:S(2)}) async-start(bf16[8,32,1024]{2,1,0:T(8,128)(2,1)} %bitcast.25), calls=%async_computation.2 | async-start | bytes 1048576 | tf_op jit(solution)/shard_map/all_to_all | solution.py:34
  57.7 9.9 %collective-permute-start = (f32[32,512]{1,0:T(8,128)S(1)}, f32[32,512]{1,0:T(8,128)S(1)}, u32[]{:S(2)}, u32[]{:S(2)}) collective-permute-start(f32[32,512]{1,0:T(8,128)S(1)} %pad_maximum_fusion.2), channel_id=1, source_target_pairs={{0,256},{256,0},{1,257},{257,1},{2,258},{258,2},{3,259},{259,3},{4... | collective-permute-start | bytes 196616 | tf_op jit(solution)/shard_map/ppermute | solution.py:103
  68.5 14.2 %all-to-all-start.3 = ((bf16[8,32,1024]{2,1,0:T(8,128)(2,1)}), bf16[8,32,1024]{2,1,0:T(8,128)(2,1)S(1)}, u32[]{:S(2)}, u32[]{:S(2)}) async-start(bf16[8,32,1024]{2,1,0:T(8,128)(2,1)} %broadcast_in_dim.9), calls=%async_computation.3 | async-start | bytes 1048576 | tf_op jit(solution)/shard_map/all_to_all | solution.py:34
  73.5 8.2 %collective-permute-start.3 = (bf16[32,256]{1,0:T(8,128)(2,1)S(1)}, bf16[32,256]{1,0:T(8,128)(2,1)S(1)}, u32[]{:S(2)}, u32[]{:S(2)}) collective-permute-start(bf16[32,256]{1,0:T(8,128)(2,1)S(1)} %get-tuple-element.50), channel_id=1, source_target_pairs={{0,1},{1,0},{2,3},{3,2},{4,5},{5,4},{6,7},{7,6},{8,9},{9,8},{10,11... | collective-permute-start | bytes 49160 | tf_op jit(solution)/shard_map/ppermute | solution.py:113
  83.4 12.1 %collective-permute-start.4 = (bf16[256,1024]{1,0:T(8,128)(2,1)S(1)}, bf16[256,1024]{1,0:T(8,128)(2,1)S(1)}, u32[]{:S(2)}, u32[]{:S(2)}) collective-permute-start(bf16[256,1024]{1,0:T(8,128)(2,1)S(1)} %bitcast.19), channel_id=1, source_target_pairs={{0,256},{256,0},{1,257},{257,1},{2,258},{258,2},{3,259},{259,3},{4... | collective-permute-start | bytes 1572872 | tf_op jit(solution)/shard_map/ppermute | solution.py:119
  87.8 13.4 %all-to-all-start.5 = ((bf16[8,32,512]{2,1,0:T(8,128)(2,1)}), bf16[8,32,512]{2,1,0:T(8,128)(2,1)S(1)}, u32[]{:S(2)}, u32[]{:S(2)}) async-start(bf16[8,32,512]{2,1,0:T(8,128)(2,1)} %broadcast_in_dim.10), calls=%async_computation.5 | async-start | bytes 524288 | tf_op jit(solution)/shard_map/all_to_all | solution.py:34
  93.7 1.8 %copy-start.2 = (bf16[512,1024]{1,0:T(8,128)(2,1)S(1)}, bf16[512,1024]{1,0:T(8,128)(2,1)}, u32[]{:S(2)}) copy-start(bf16[512,1024]{1,0:T(8,128)(2,1)} %copy-done.1) | copy-start | bytes 3145732
  101.2 28.5 %all-to-all-start.4 = ((bf16[16,16,512]{2,1,0:T(8,128)(2,1)}), bf16[16,16,512]{2,1,0:T(8,128)(2,1)}, u32[]{:S(2)}, u32[]{:S(2)}) async-start(bf16[16,16,512]{2,1,0:T(8,128)(2,1)} %bitcast.26), calls=%async_computation.4 | async-start | bytes 524288 | tf_op jit(solution)/shard_map/all_to_all | solution.py:34
  114.6 11.4 %collective-permute-start.7 = (bf16[256,512]{1,0:T(8,128)(2,1)S(1)}, bf16[256,512]{1,0:T(8,128)(2,1)S(1)}, u32[]{:S(2)}, u32[]{:S(2)}) collective-permute-start(bf16[256,512]{1,0:T(8,128)(2,1)S(1)} %bitcast.23), channel_id=1, source_target_pairs={{0,256},{256,0},{1,257},{257,1},{2,258},{258,2},{3,259},{259,3},{4... | collective-permute-start | bytes 786440 | tf_op jit(solution)/shard_map/ppermute | solution.py:117
  119.0 7.0 %collective-permute-start.5 = (bf16[256,512]{1,0:T(8,128)(2,1)S(1)}, bf16[256,512]{1,0:T(8,128)(2,1)S(1)}, u32[]{:S(2)}, u32[]{:S(2)}) collective-permute-start(bf16[256,512]{1,0:T(8,128)(2,1)S(1)} %slice.54), channel_id=1, source_target_pairs={{0,1},{1,0},{2,3},{3,2},{4,5},{5,4},{6,7},{7,6},{8,9},{9,8},{10,11... | collective-permute-start | bytes 786440 | tf_op jit(solution)/shard_map/ppermute | solution.py:125
  124.1 3.4 %collective-permute-start.6 = (bf16[256,512]{1,0:T(8,128)(2,1)S(1)}, bf16[256,512]{1,0:T(8,128)(2,1)S(1)}, u32[]{:S(2)}, u32[]{:S(2)}) collective-permute-start(bf16[256,512]{1,0:T(8,128)(2,1)S(1)} %slice.55), channel_id=1, source_target_pairs={{0,1},{1,0},{2,3},{3,2},{4,5},{5,4},{6,7},{7,6},{8,9},{9,8},{10,11... | collective-permute-start | bytes 786440 | tf_op jit(solution)/shard_map/ppermute | solution.py:126

commit v6 on v5

--- a/solution.py
+++ b/solution.py
@@ -25,7 +25,7 @@
     return lax.dot_general(a, b, dims, preferred_element_type=f32)
 
 
-Z_ORDER = (0, 4, 7, 3, 1, 5, 6, 2)
+Z_ORDER = (0, 4, 6, 7, 2, 5, 1, 3)
 COL_ORDER = (0, 2, 4, 6, 8, 10, 12, 14, 1, 3, 5, 7, 9, 11, 13, 15)
 
 

time: 132 us -> 132 us (level)
  waiting for transfers between devices: 27.1 us -> 24.6 us
  starting transfers between devices: 87.1 us -> 89.5 us
    all_to_all x6, waiting for transfers between devices: 21.3 us -> 18.9 us  [exchange(): lax.all_to_all(x, axis, 0, 0, tiled=True, axis_index_groups=[list(order)])]
    all_to_all x6, starting transfers between devices: 50 us -> 52.3 us  [exchange(): lax.all_to_all(x, axis, 0, 0, tiled=True, axis_index_groups=[list(order)])]
    ppermute x1, starting transfers between devices: 5.03 us -> 6.71 us  [body(): other_own = lax.ppermute(own_gu[:, 512:], 'dp', SWAP)]
where the time goes in v6:
time: 132 us; the launch traced here: 131 us
  starting transfers between devices  89.5 us (68%)
  waiting for transfers between devices  24.6 us (19%)
  matrix products  5.12 us (4%)
  other arithmetic  4.92 us (4%)
  local copies, waits for them, and re-layouts  3.95 us (3%)
  Pallas kernels  2.14 us (2%)
    all_to_all x6, starting transfers between devices, exchange(): lax.all_to_all(x, axis, 0, 0, tiled=True, axis_index_groups=[list(order)])  52.3 us
    all_to_all x6, waiting for transfers between devices, exchange(): lax.all_to_all(x, axis, 0, 0, tiled=True, axis_index_groups=[list(order)])  18.9 us
    ppermute x1, starting transfers between devices, body(): other_own = lax.ppermute(own_gu[:, 512:], 'dp', SWAP)  6.71 us
    ppermute x1, starting transfers between devices, body(): lax.ppermute(hidden[:, 256:], 'dp', SWAP)  6.49 us
    ppermute x1, starting transfers between devices, body(): other = lax.ppermute(own, 'dp', SWAP)  5.37 us
    dot_general x5, matrix products, dot(): return lax.dot_general(a, b, dims, preferred_element_type=f32)  5.12 us
    ppermute x1, starting transfers between devices, body(): gh = grad_hidden(x_hi) + lax.ppermute(grad_hidden(1 - x_hi), 'x_hi', SWAP)  4.36 us
    ppermute x1, starting transfers between devices, body(): got = lax.ppermute(dot(own_in, gu_send, PLAIN).astype(bf16), 'x_hi', SWAP)  4.36 us
  transfers between devices with their start and end apart: 14, of which 7 were waited for; matrix products, arithmetic and copies ran while one was open for 6% of the time, Pallas kernels for 2%

profile of v6, /device:TPU:1, one launch (start us, length us, event | category | flops | bytes accessed | tf_op | source)
XLA Modules:
  0.0 131.2 jit_solution(1691942746399214256)
XLA Ops:
  0.6 0.0 copy-start
  0.6 0.0 copy-start.4
  0.7 0.9 pad_maximum_fusion.6
  1.5 0.9 broadcast_in_dim.8
  2.4 8.7 %all-to-all-start = ((bf16[16,16,1024]{2,1,0:T(8,128)(2,1)}), bf16[16,16,1024]{2,1,0:T(8,128)(2,1)S(1)}, u32[]{:S(2)}, u32[]{:S(2)}) async-start(bf16[16,16,1024]{2,1,0:T(8,128)(2,1)} %broadcast_in_dim.8), calls=%async_computation | async-start | bytes 1048576 | tf_op jit(solution)/shard_map/all_to_all | solution.py:34
  11.1 0.0 copy-done.4
  11.1 1.4 %constant_dynamic-slice_fusion.6 = (bf16[512,256]{1,0:T(8,128)(2,1)S(1)}, bf16[512,256]{1,0:T(8,128)(2,1)S(1)}, bf16[512,256]{1,0:T(8,128)(2,1)S(1)}, bf16[512,2...) fusion(bf16[512,1024]{1,0:T(8,128)(2,1)S(1)} %copy-done.4, ...), kind=kLoop, calls=%fused_computation.30 | loop fusion | bytes 4194320 | tf_op jit(solution)/shard_map/dynamic_slice | solution.py:85
  12.5 1.1 pad_maximum_fusion
  13.7 0.1 pad_maximum_fusion.1
  13.8 0.0 copy-start.1
  13.8 10.5 %all-to-all-done = bf16[16,16,1024]{2,1,0:T(8,128)(2,1)S(1)} async-done(((bf16[16,16,1024]{2,1,0:T(8,128)(2,1)}), bf16[16,16,1024]{2,1,0:T(8,128)(2,1)S(1)}, u32[]{:S(2)}, u32[]{:S(2)}) %all-to-all-start) | async-done | bytes 524320 | tf_op jit(solution)/shard_map/all_to_all | solution.py:34
  24.3 0.0 copy-done
  24.3 1.3 convolution_convert_fusion.1
  25.5 10.6 %all-to-all-start.1 = ((bf16[8,32,1024]{2,1,0:T(8,128)(2,1)}), bf16[8,32,1024]{2,1,0:T(8,128)(2,1)S(1)}, u32[]{:S(2)}, u32[]{:S(2)}) async-start(bf16[8,32,1024]{2,1,0:T(8,128)(2,1)} %bitcast.1), calls=%async_computation.1 | async-start | bytes 1048576 | tf_op jit(solution)/shard_map/all_to_all | solution.py:34
  36.1 0.0 copy-done.1
  36.1 0.0 copy-start.3
  36.2 0.4 convolution_convert_fusion
  36.6 4.4 %collective-permute-start.1 = (bf16[256,1024]{1,0:T(8,128)(2,1)S(1)}, bf16[256,1024]{1,0:T(8,128)(2,1)S(1)}, u32[]{:S(2)}, u32[]{:S(2)}) collective-permute-start(bf16[256,1024]{1,0:T(8,128)(2,1)S(1)} %convolution_convert_fusion), channel_id=1, source_target_pairs={{0,256},{256,0},{1,257},{257,1},{2,258},{258,2},{3,259},{259,3},{4... | collective-permute-start | bytes 1572872 | tf_op jit(solution)/shard_map/ppermute | solution.py:97
  41.0 5.4 %collective-permute-start.2 = (bf16[256,1024]{1,0:T(8,128)(2,1)S(1)}, bf16[256,1024]{1,0:T(8,128)(2,1)S(1)}, u32[]{:S(2)}, u32[]{:S(2)}) collective-permute-start(bf16[256,1024]{1,0:T(8,128)(2,1)S(1)} %bitcast.16), channel_id=1, source_target_pairs={{0,1},{1,0},{2,3},{3,2},{4,5},{5,4},{6,7},{7,6},{8,9},{9,8},{10,11... | collective-permute-start | bytes 1572872 | tf_op jit(solution)/shard_map/ppermute | solution.py:104
  46.3 0.0 copy-done.3
  46.4 0.4 fusion.3
  46.8 3.4 %collective-permute-done.1 = bf16[256,1024]{1,0:T(8,128)(2,1)S(1)} collective-permute-done((bf16[256,1024]{1,0:T(8,128)(2,1)S(1)}, bf16[256,1024]{1,0:T(8,128)(2,1)S(1)}, u32[]{:S(2)}, u32[]{:S(2)}) %collective-permute-start.1) | collective-permute-done | bytes 524320 | tf_op jit(solution)/shard_map/ppermute | solution.py:97
  50.2 0.0 collective-permute-done.2.other
  50.2 0.9 add_convert_fusion
  51.2 0.0 all-to-all-done.1
  51.2 6.4 %all-to-all-start.2 = ((bf16[8,32,1024]{2,1,0:T(8,128)(2,1)}), bf16[8,32,1024]{2,1,0:T(8,128)(2,1)S(1)}, u32[]{:S(2)}, u32[]{:S(2)}) async-start(bf16[8,32,1024]{2,1,0:T(8,128)(2,1)} %bitcast.25), calls=%async_computation.2 | async-start | bytes 1048576 | tf_op jit(solution)/shard_map/all_to_all | solution.py:34
  57.5 0.1 convert_reduce_fusion.1
  57.7 4.4 %collective-permute-start = (f32[32,512]{1,0:T(8,128)S(1)}, f32[32,512]{1,0:T(8,128)S(1)}, u32[]{:S(2)}, u32[]{:S(2)}) collective-permute-start(f32[32,512]{1,0:T(8,128)S(1)} %pad_maximum_fusion.2), channel_id=1, source_target_pairs={{0,256},{256,0},{1,257},{257,1},{2,258},{258,2},{3,259},{259,3},{4... | collective-permute-start | bytes 196616 | tf_op jit(solution)/shard_map/ppermute | solution.py:103
  62.0 3.5 %all-to-all-done.2 = bf16[8,32,1024]{2,1,0:T(8,128)(2,1)S(1)} async-done(((bf16[8,32,1024]{2,1,0:T(8,128)(2,1)}), bf16[8,32,1024]{2,1,0:T(8,128)(2,1)S(1)}, u32[]{:S(2)}, u32[]{:S(2)}) %all-to-all-start.2) | async-done | bytes 524320 | tf_op jit(solution)/shard_map/all_to_all | solution.py:34
  65.6 0.1 convert_reduce_fusion
  65.7 0.0 collective-permute-done
  65.7 0.1 multiply_convert_fusion.2
  65.8 0.9 broadcast_in_dim.9
  66.6 7.9 %all-to-all-start.3 = ((bf16[8,32,1024]{2,1,0:T(8,128)(2,1)}), bf16[8,32,1024]{2,1,0:T(8,128)(2,1)S(1)}, u32[]{:S(2)}, u32[]{:S(2)}) async-start(bf16[8,32,1024]{2,1,0:T(8,128)(2,1)} %broadcast_in_dim.9), calls=%async_computation.3 | async-start | bytes 1048576 | tf_op jit(solution)/shard_map/all_to_all | solution.py:34
  74.6 6.5 %collective-permute-start.3 = (bf16[32,256]{1,0:T(8,128)(2,1)S(1)}, bf16[32,256]{1,0:T(8,128)(2,1)S(1)}, u32[]{:S(2)}, u32[]{:S(2)}) collective-permute-start(bf16[32,256]{1,0:T(8,128)(2,1)S(1)} %get-tuple-element.50), channel_id=1, source_target_pairs={{0,1},{1,0},{2,3},{3,2},{4,5},{5,4},{6,7},{7,6},{8,9},{9,8},{10,11... | collective-permute-start | bytes 49160 | tf_op jit(solution)/shard_map/ppermute | solution.py:113
  81.1 0.8 collective-permute-done.3
  81.9 0.7 all-to-all-done.3
  82.6 0.7 broadcast_in_dim.10
  83.4 4.4 %collective-permute-start.4 = (bf16[256,1024]{1,0:T(8,128)(2,1)S(1)}, bf16[256,1024]{1,0:T(8,128)(2,1)S(1)}, u32[]{:S(2)}, u32[]{:S(2)}) collective-permute-start(bf16[256,1024]{1,0:T(8,128)(2,1)S(1)} %bitcast.19), channel_id=1, source_target_pairs={{0,256},{256,0},{1,257},{257,1},{2,258},{258,2},{3,259},{259,3},{4... | collective-permute-start | bytes 1572872 | tf_op jit(solution)/shard_map/ppermute | solution.py:119
  87.7 8.0 %all-to-all-start.5 = ((bf16[8,32,512]{2,1,0:T(8,128)(2,1)}), bf16[8,32,512]{2,1,0:T(8,128)(2,1)S(1)}, u32[]{:S(2)}, u32[]{:S(2)}) async-start(bf16[8,32,512]{2,1,0:T(8,128)(2,1)} %broadcast_in_dim.10), calls=%async_computation.5 | async-start | bytes 524288 | tf_op jit(solution)/shard_map/all_to_all | solution.py:34
  95.8 0.0 copy-start.2
  95.8 1.8 %fusion.9 = f32[256,512]{1,0:T(8,128)S(1)} fusion(bf16[256,1024]{1,0:T(8,128)(2,1)S(1)} %bitcast.20, bf16[512,1024]{1,0:T(8,128)(2,1)} %pad_maximum_fusion), kind=kOutput, calls=%fused_computation.40 | convolution fusion | flops 268435456 | bytes 2097152 | tf_op jit(solution)/shard_map/dot_general | solution.py:25
  97.6 0.0 collective-permute-done.4.far_gu
  97.6 0.0 copy-done.2
  97.6 1.2 fusion
  98.8 4.1 %all-to-all-done.5 = bf16[8,32,512]{2,1,0:T(8,128)(2,1)S(1)} async-done(((bf16[8,32,512]{2,1,0:T(8,128)(2,1)}), bf16[8,32,512]{2,1,0:T(8,128)(2,1)S(1)}, u32[]{:S(2)}, u32[]{:S(2)}) %all-to-all-start.5) | async-done | bytes 262176 | tf_op jit(solution)/shard_map/all_to_all | solution.py:34
  102.9 10.7 %all-to-all-start.4 = ((bf16[16,16,512]{2,1,0:T(8,128)(2,1)}), bf16[16,16,512]{2,1,0:T(8,128)(2,1)}, u32[]{:S(2)}, u32[]{:S(2)}) async-start(bf16[16,16,512]{2,1,0:T(8,128)(2,1)} %bitcast.26), calls=%async_computation.4 | async-start | bytes 524288 | tf_op jit(solution)/shard_map/all_to_all | solution.py:34
  113.6 3.6 %collective-permute-start.7 = (bf16[256,512]{1,0:T(8,128)(2,1)S(1)}, bf16[256,512]{1,0:T(8,128)(2,1)S(1)}, u32[]{:S(2)}, u32[]{:S(2)}) collective-permute-start(bf16[256,512]{1,0:T(8,128)(2,1)S(1)} %bitcast.23), channel_id=1, source_target_pairs={{0,256},{256,0},{1,257},{257,1},{2,258},{258,2},{3,259},{259,3},{4... | collective-permute-start | bytes 786440 | tf_op jit(solution)/shard_map/ppermute | solution.py:117
  117.3 6.7 %collective-permute-start.5 = (bf16[256,512]{1,0:T(8,128)(2,1)S(1)}, bf16[256,512]{1,0:T(8,128)(2,1)S(1)}, u32[]{:S(2)}, u32[]{:S(2)}) collective-permute-start(bf16[256,512]{1,0:T(8,128)(2,1)S(1)} %slice.54), channel_id=1, source_target_pairs={{0,1},{1,0},{2,3},{3,2},{4,5},{5,4},{6,7},{7,6},{8,9},{9,8},{10,11... | collective-permute-start | bytes 786440 | tf_op jit(solution)/shard_map/ppermute | solution.py:125
  124.0 1.9 %collective-permute-start.6 = (bf16[256,512]{1,0:T(8,128)(2,1)S(1)}, bf16[256,512]{1,0:T(8,128)(2,1)S(1)}, u32[]{:S(2)}, u32[]{:S(2)}) collective-permute-start(bf16[256,512]{1,0:T(8,128)(2,1)S(1)} %slice.55), channel_id=1, source_target_pairs={{0,1},{1,0},{2,3},{3,2},{4,5},{5,4},{6,7},{7,6},{8,9},{9,8},{10,11... | collective-permute-start | bytes 786440 | tf_op jit(solution)/shard_map/ppermute | solution.py:126
  125.9 0.0 collective-permute-done.7.far_h
  126.0 0.0 collective-permute-done.5.other_own
  126.0 1.5 %collective-permute-done.6.other_far = bf16[256,512]{1,0:T(8,128)(2,1)S(1)} collective-permute-done((bf16[256,512]{1,0:T(8,128)(2,1)S(1)}, bf16[256,512]{1,0:T(8,128)(2,1)S(1)}, u32[]{:S(2)}, u32[]{:S(2)}) %collective-permute-start.6) | collective-permute-done | bytes 262176 | tf_op jit(solution)/shard_map/ppermute | solution.py:126
  127.4 2.1 %shard_map.84 = (bf16[512,512]{1,0:T(8,128)(2,1)}, bf16[512,512]{1,0:T(8,128)(2,1)}, bf16[512,512]{1,0:T(8,128)(2,1)}) custom-call(s32[1]{0:T(128)} %bitcast.5.x_hi, bf16[256,1024]{1,0:T(8,128)(2,1)S(1)} %bitcast.18, bf16[256,1024]{1,0:T(8,128)(2,1)S(1)} %collective-permute-done.2.other, bf16[256,1024]{1,0:T(8,128)(2,1)S(1)} %bitcast.22, ...), custom_call_target="tpu_custom_call" | custom-call | flops 805306368 | bytes 5242880 | tf_op jit(solution)/shard_map/pallas_call | solution.py:68
  129.6 0.0 all-to-all-done.4
  129.6 1.6 %reduce_sum.32 = bf16[16,512]{1,0:T(8,128)(2,1)} reduce(bf16[16,16,512]{2,1,0:T(8,128)(2,1)} %all-to-all-done.4, bf16[]{:T(256)} %constant.23.clone.1), dimensions={0}, to_apply=%region_2.0 | reduce | flops 122880 | bytes 278530 | tf_op jit(solution)/shard_map/reduce_sum | solution.py:45
  (10 shorter events, 0.1 us)
Async XLA Ops:
  0.6 23.6 %copy-start = (bf16[1024,512]{1,0:T(8,128)(2,1)S(1)}, bf16[1024,512]{1,0:T(8,128)(2,1)}, u32[]{:S(2)}) copy-start(bf16[1024,512]{1,0:T(8,128)(2,1)} %param.9) | copy-start | bytes 3145732
  0.6 10.5 %copy-start.4 = (bf16[512,1024]{1,0:T(8,128)(2,1)S(1)}, bf16[512,1024]{1,0:T(8,128)(2,1)}, u32[]{:S(2)}) copy-start(bf16[512,1024]{1,0:T(8,128)(2,1)} %param.8) | copy-start | bytes 3145732
  2.4 21.9 %all-to-all-start = ((bf16[16,16,1024]{2,1,0:T(8,128)(2,1)}), bf16[16,16,1024]{2,1,0:T(8,128)(2,1)S(1)}, u32[]{:S(2)}, u32[]{:S(2)}) async-start(bf16[16,16,1024]{2,1,0:T(8,128)(2,1)} %broadcast_in_dim.8), calls=%async_computation | async-start | bytes 1048576 | tf_op jit(solution)/shard_map/all_to_all | solution.py:34
  13.8 22.3 %copy-start.1 = (bf16[512,1024]{1,0:T(8,128)(2,1)}, bf16[512,1024]{1,0:T(8,128)(2,1)S(1)}, u32[]{:S(2)}) copy-start(bf16[512,1024]{1,0:T(8,128)(2,1)S(1)} %pad_maximum_fusion.1) | copy-start | bytes 3145732
  25.5 25.6 %all-to-all-start.1 = ((bf16[8,32,1024]{2,1,0:T(8,128)(2,1)}), bf16[8,32,1024]{2,1,0:T(8,128)(2,1)S(1)}, u32[]{:S(2)}, u32[]{:S(2)}) async-start(bf16[8,32,1024]{2,1,0:T(8,128)(2,1)} %bitcast.1), calls=%async_computation.1 | async-start | bytes 1048576 | tf_op jit(solution)/shard_map/all_to_all | solution.py:34
  36.1 10.2 %copy-start.3 = (bf16[512,1024]{1,0:T(8,128)(2,1)S(1)}, bf16[512,1024]{1,0:T(8,128)(2,1)}, u32[]{:S(2)}) copy-start(bf16[512,1024]{1,0:T(8,128)(2,1)} %pad_maximum_fusion) | copy-start | bytes 3145732
  36.6 13.6 %collective-permute-start.1 = (bf16[256,1024]{1,0:T(8,128)(2,1)S(1)}, bf16[256,1024]{1,0:T(8,128)(2,1)S(1)}, u32[]{:S(2)}, u32[]{:S(2)}) collective-permute-start(bf16[256,1024]{1,0:T(8,128)(2,1)S(1)} %convolution_convert_fusion), channel_id=1, source_target_pairs={{0,256},{256,0},{1,257},{257,1},{2,258},{258,2},{3,259},{259,3},{4... | collective-permute-start | bytes 1572872 | tf_op jit(solution)/shard_map/ppermute | solution.py:97
  41.0 9.3 %collective-permute-start.2 = (bf16[256,1024]{1,0:T(8,128)(2,1)S(1)}, bf16[256,1024]{1,0:T(8,128)(2,1)S(1)}, u32[]{:S(2)}, u32[]{:S(2)}) collective-permute-start(bf16[256,1024]{1,0:T(8,128)(2,1)S(1)} %bitcast.16), channel_id=1, source_target_pairs={{0,1},{1,0},{2,3},{3,2},{4,5},{5,4},{6,7},{7,6},{8,9},{9,8},{10,11... | collective-permute-start | bytes 1572872 | tf_op jit(solution)/shard_map/ppermute | solution.py:104
  51.2 14.4 %all-to-all-start.2 = ((bf16[8,32,1024]{2,1,0:T(8,128)(2,1)}), bf16[8,32,1024]{2,1,0:T(8,128)(2,1)S(1)}, u32[]{:S(2)}, u32[]{:S(2)}) async-start(bf16[8,32,1024]{2,1,0:T(8,128)(2,1)} %bitcast.25), calls=%async_computation.2 | async-start | bytes 1048576 | tf_op jit(solution)/shard_map/all_to_all | solution.py:34
  57.7 8.0 %collective-permute-start = (f32[32,512]{1,0:T(8,128)S(1)}, f32[32,512]{1,0:T(8,128)S(1)}, u32[]{:S(2)}, u32[]{:S(2)}) collective-permute-start(f32[32,512]{1,0:T(8,128)S(1)} %pad_maximum_fusion.2), channel_id=1, source_target_pairs={{0,256},{256,0},{1,257},{257,1},{2,258},{258,2},{3,259},{259,3},{4... | collective-permute-start | bytes 196616 | tf_op jit(solution)/shard_map/ppermute | solution.py:103
  66.6 16.0 %all-to-all-start.3 = ((bf16[8,32,1024]{2,1,0:T(8,128)(2,1)}), bf16[8,32,1024]{2,1,0:T(8,128)(2,1)S(1)}, u32[]{:S(2)}, u32[]{:S(2)}) async-start(bf16[8,32,1024]{2,1,0:T(8,128)(2,1)} %broadcast_in_dim.9), calls=%async_computation.3 | async-start | bytes 1048576 | tf_op jit(solution)/shard_map/all_to_all | solution.py:34
  74.6 7.3 %collective-permute-start.3 = (bf16[32,256]{1,0:T(8,128)(2,1)S(1)}, bf16[32,256]{1,0:T(8,128)(2,1)S(1)}, u32[]{:S(2)}, u32[]{:S(2)}) collective-permute-start(bf16[32,256]{1,0:T(8,128)(2,1)S(1)} %get-tuple-element.50), channel_id=1, source_target_pairs={{0,1},{1,0},{2,3},{3,2},{4,5},{5,4},{6,7},{7,6},{8,9},{9,8},{10,11... | collective-permute-start | bytes 49160 | tf_op jit(solution)/shard_map/ppermute | solution.py:113
  83.4 14.2 %collective-permute-start.4 = (bf16[256,1024]{1,0:T(8,128)(2,1)S(1)}, bf16[256,1024]{1,0:T(8,128)(2,1)S(1)}, u32[]{:S(2)}, u32[]{:S(2)}) collective-permute-start(bf16[256,1024]{1,0:T(8,128)(2,1)S(1)} %bitcast.19), channel_id=1, source_target_pairs={{0,256},{256,0},{1,257},{257,1},{2,258},{258,2},{3,259},{259,3},{4... | collective-permute-start | bytes 1572872 | tf_op jit(solution)/shard_map/ppermute | solution.py:119
  87.7 15.2 %all-to-all-start.5 = ((bf16[8,32,512]{2,1,0:T(8,128)(2,1)}), bf16[8,32,512]{2,1,0:T(8,128)(2,1)S(1)}, u32[]{:S(2)}, u32[]{:S(2)}) async-start(bf16[8,32,512]{2,1,0:T(8,128)(2,1)} %broadcast_in_dim.10), calls=%async_computation.5 | async-start | bytes 524288 | tf_op jit(solution)/shard_map/all_to_all | solution.py:34
  95.8 1.8 %copy-start.2 = (bf16[512,1024]{1,0:T(8,128)(2,1)S(1)}, bf16[512,1024]{1,0:T(8,128)(2,1)}, u32[]{:S(2)}) copy-start(bf16[512,1024]{1,0:T(8,128)(2,1)} %copy-done.1) | copy-start | bytes 3145732
  102.9 26.7 %all-to-all-start.4 = ((bf16[16,16,512]{2,1,0:T(8,128)(2,1)}), bf16[16,16,512]{2,1,0:T(8,128)(2,1)}, u32[]{:S(2)}, u32[]{:S(2)}) async-start(bf16[16,16,512]{2,1,0:T(8,128)(2,1)} %bitcast.26), calls=%async_computation.4 | async-start | bytes 524288 | tf_op jit(solution)/shard_map/all_to_all | solution.py:34
  113.6 12.3 %collective-permute-start.7 = (bf16[256,512]{1,0:T(8,128)(2,1)S(1)}, bf16[256,512]{1,0:T(8,128)(2,1)S(1)}, u32[]{:S(2)}, u32[]{:S(2)}) collective-permute-start(bf16[256,512]{1,0:T(8,128)(2,1)S(1)} %bitcast.23), channel_id=1, source_target_pairs={{0,256},{256,0},{1,257},{257,1},{2,258},{258,2},{3,259},{259,3},{4... | collective-permute-start | bytes 786440 | tf_op jit(solution)/shard_map/ppermute | solution.py:117
  117.3 8.7 %collective-permute-start.5 = (bf16[256,512]{1,0:T(8,128)(2,1)S(1)}, bf16[256,512]{1,0:T(8,128)(2,1)S(1)}, u32[]{:S(2)}, u32[]{:S(2)}) collective-permute-start(bf16[256,512]{1,0:T(8,128)(2,1)S(1)} %slice.54), channel_id=1, source_target_pairs={{0,1},{1,0},{2,3},{3,2},{4,5},{5,4},{6,7},{7,6},{8,9},{9,8},{10,11... | collective-permute-start | bytes 786440 | tf_op jit(solution)/shard_map/ppermute | solution.py:125
  124.0 3.4 %collective-permute-start.6 = (bf16[256,512]{1,0:T(8,128)(2,1)S(1)}, bf16[256,512]{1,0:T(8,128)(2,1)S(1)}, u32[]{:S(2)}, u32[]{:S(2)}) collective-permute-start(bf16[256,512]{1,0:T(8,128)(2,1)S(1)} %slice.55), channel_id=1, source_target_pairs={{0,1},{1,0},{2,3},{3,2},{4,5},{5,4},{6,7},{7,6},{8,9},{9,8},{10,11... | collective-permute-start | bytes 786440 | tf_op jit(solution)/shard_map/ppermute | solution.py:126
